TPU v7x, 32 devices: a whole 2x2x4 slice. The times are simulated.
32 devices in a mesh: space: 8 (over y, x, core), filt: 4 (over z).
Axes of the slice: x: 2, y: 2, z: 4, core: 2. Of those that a mesh axis runs over, the one named last changes fastest.
Arguments:
- volume: bfloat16 [32, 64, 16, 128], P('space', 'filt'), may hold values from -6 to 6
- w_early: bfloat16 [27, 128, 128], replicated, may hold values from -0.109375 to 0.109375
- w_deep: bfloat16 [27, 128, 256], P(None, None, 'filt'), may hold values from -0.109375 to 0.109375
- cotangent: bfloat16 [16, 32, 8, 256], P('space', None, None, 'filt'), may hold values from -6 to 6
Outputs:
- block_out: bfloat16 [16, 32, 8, 256], P('space', None, None, 'filt')
- grad_early: float32 [27, 128, 128], replicated
- grad_deep: float32 [27, 128, 256], P(None, None, 'filt')
All inputs are finite; a program needn't handle non-finite values.
Results may differ from a plain program's by a relative error of at most 0.0059.
Values may be sent and summed in bfloat16 or wider, within the bound.
No kernel may reach another device: no remote copies, remote signals or barrier semaphores. Data moves between devices by JAX's collectives and lax.ppermute only.
A program may use at most 128 MiB of HBM per device.

v0:
```python
import functools
import math

import jax
import jax.numpy as jnp
from jax import lax
from jax.experimental import pallas as pl
from jax.experimental.pallas import tpu as pltpu
from jax.sharding import PartitionSpec as P

F32 = jnp.float32
BF16 = jnp.bfloat16
VMEM_LIMIT = 24 * 1024 * 1024
VMEM = pl.BlockSpec(memory_space=pltpu.VMEM)
HBM = pl.BlockSpec(memory_space=pltpu.HBM)
DMA = pltpu.SemaphoreType.DMA


def call(
    body, name, out_shape, operands, scratch=(), flops=0, moved=1 << 20, hbm=(), outs=VMEM, alias=()
):
    return pl.pallas_call(
        body,
        name=name,
        out_shape=out_shape,
        in_specs=[HBM if i in hbm else VMEM for i in range(len(operands))],
        out_specs=jax.tree.map(lambda _: outs, out_shape),
        scratch_shapes=list(scratch),
        input_output_aliases=dict(alias),
        compiler_params=pltpu.CompilerParams(vmem_limit_bytes=VMEM_LIMIT),
        cost_estimate=pl.CostEstimate(flops=flops, bytes_accessed=moved, transcendentals=0),
    )(*operands)


def struct(shape, dtype=BF16):
    return jax.ShapeDtypeStruct(shape, dtype)


def ceil_to(value, step):
    return -(-value // step) * step


def sigmoid(value):
    return 1.0 / (1.0 + jnp.exp(-value))


def sides_body(ylo, yhi, sides):
    sides[:, 0:1] = ylo[...]
    sides[:, 1:2] = yhi[...]


def early_body(
    volume, xlo, xhi, ylo, yhi, clo, chi, w, windows, sg, pooled, center, field, wide, sem, wsem
):
    nx, ny, nz, cin = volume.shape
    cout = w.shape[3]
    half = nz // 2
    rows = ny * half
    ext = nx + 6
    space = lax.axis_size("space")
    fetch = pltpu.make_async_copy(volume, center, sem.at[0])
    fetch.start()
    weights = [
        pltpu.make_async_copy(
            w.at[pl.ds(3 * a, 3), tap],
            wide.at[
                pl.ds(3 * a, 3),
                pl.ds((tap + side) * cin, cin),
                pl.ds(side * cout, cout),
            ],
            wsem.at[a, 2 * tap + side],
        )
        for a in range(3)
        for tap in range(3)
        for side in range(2)
    ]
    for copy in weights:
        copy.start()
    wide[:, 0:cin, cout:] = jnp.zeros((9, cin, cout), BF16)
    wide[:, 3 * cin :, :cout] = jnp.zeros((9, cin, cout), BF16)
    field[:, :, 0:8] = jnp.zeros((ext, ny + 2, 8, cin), F32)
    field[:, :, 8 + nz : 16 + nz] = jnp.zeros((ext, ny + 2, 8, cin), F32)
    cells = slice(8, 8 + nz)
    for top, size, main, sides in ((0, 3, xlo, clo), (nx + 3, 3, xhi, chi)):
        first = nx - 3 if top == 0 else 0
        field[top : top + size, 1 : ny + 1, cells] = main[first : first + size].astype(F32)
        field[top : top + size, 0:1, cells] = sides[first : first + size, 0:1].astype(F32)
        field[top : top + size, ny + 1 :, cells] = sides[first : first + size, 1:2].astype(F32)
    field[3 : nx + 3, 0:1, cells] = ylo[...].astype(F32)
    field[3 : nx + 3, ny + 1 :, cells] = yhi[...].astype(F32)
    fetch.wait()
    field[3 : nx + 3, 1 : ny + 1, cells] = center[...].astype(F32)
    for x in range(ext):
        for group in range(4):
            plane = field[x, :, pl.ds(7 + group, half, stride=2), :]
            for b in range(3):
                windows[b, x, :, group * cin : (group + 1) * cin] = (
                    plane[b : b + ny].reshape(rows, cin).astype(BF16)
                )
    low = jnp.where(lax.axis_index("space") > 0, 1.0, 0.0).astype(F32)
    high = jnp.where(lax.axis_index("space") < space - 1, 1.0, 0.0).astype(F32)
    for chunk in range(nx // 2 + 2):
        start = 2 * chunk
        acc = jnp.zeros((2 * rows, 2 * cout), F32)
        for ab in range(9):
            a, b = ab // 3, ab % 3
            if chunk == 0 and b == 0:
                for copy in weights[6 * a : 6 * a + 6]:
                    copy.wait()
            left = windows[b, start + a : start + a + 2].reshape(2 * rows, 4 * cin)
            acc = acc + jnp.dot(left, wide[ab], preferred_element_type=F32)
        sig = sigmoid(acc)
        keep = 0.125
        if chunk == 0:
            keep = 0.125 * low
        if chunk == nx // 2 + 1:
            keep = 0.125 * high
        sg[start : start + 2] = (sig * (1.0 + acc * (1.0 - sig)) * keep).reshape(
            2, rows, 2 * cout
        )
        act = acc * sig
        act = act[:rows] + act[rows:]
        act = act[:, :cout] + act[:, cout:]
        act = act.reshape(ny // 2, 2, half, cout)
        act = (act[:, 0] + act[:, 1]) * keep
        pooled[chunk] = act.reshape(rows // 2, cout).astype(BF16)


def transpose_body(windows, turned):
    rows = windows.shape[2]
    part = turned.shape[2] // 4
    for b in range(windows.shape[0]):
        for x in range(windows.shape[1]):
            value = windows[b, x].T
            for group in range(4):
                for side in range(2):
                    spot = (2 * group + side) * part
                    turned[
                        b, side, group * part : (group + 1) * part, x * rows : (x + 1) * rows
                    ] = value[spot : spot + part]


def roll_z(value, shift):
    size = value.shape[-2]
    rolled = pltpu.roll(value, shift % size, value.ndim - 2)
    spot = lax.broadcasted_iota(jnp.int32, value.shape, value.ndim - 2)
    edge = 0 if shift == 1 else size - 1
    return jnp.where(spot == edge, 0.0, rolled)


def deep_body(parts_n, *refs):
    parts = refs[:parts_n]
    wt, cotangent = refs[parts_n : parts_n + 2]
    block_out, grad, windows = refs[parts_n + 2 : parts_n + 5]
    sends = refs[parts_n + 5 : 2 * parts_n + 5]
    field, terms, wide, cot, sem = refs[2 * parts_n + 5 :]
    nx, ny, nz, filters = cot.shape
    width = wt.shape[3]
    copies = [
        pltpu.make_async_copy(wt.at[:, c], wide.at[:, :, pl.ds(c * width, width)], sem.at[c])
        for c in range(3)
    ] + [pltpu.make_async_copy(cotangent, cot, sem.at[3])]
    for copy in copies:
        copy.start()
    rows = ny * nz
    py = ny // parts_n
    mine = lax.axis_index("filt")
    field[:, 0:1] = jnp.zeros((nx + 2, 1, nz, width), F32)
    field[:, ny + 1 : ny + 2] = jnp.zeros((nx + 2, 1, nz, width), F32)
    for j in range(parts_n):
        spot = lax.bitwise_xor(mine, j) * py + 1
        field[:, pl.ds(spot, py)] = parts[j][...].astype(F32).reshape(nx + 2, py, nz, width)
    for x in range(nx + 2):
        plane = field[x]
        for c in range(3):
            moved = plane if c == 1 else roll_z(plane, 1 - c)
            for b in range(3):
                windows[b, x, :, c * width : (c + 1) * width] = (
                    moved[b : b + ny].reshape(rows, width).astype(BF16)
                )
    for copy in copies:
        copy.wait()
    for x in range(nx):
        acc = jnp.zeros((rows, filters), F32)
        for ab in range(9):
            a, b = ab // 3, ab % 3
            acc = acc + lax.dot_general(
                windows[b, x + a], wide[ab], (((1,), (1,)), ((), ())), preferred_element_type=F32
            )
        sig = sigmoid(acc)
        block_out[x] = (acc * sig).reshape(ny, nz, filters).astype(BF16)
        slope = sig * (1.0 + acc * (1.0 - sig))
        grad[x] = (cot[x].astype(F32).reshape(rows, filters) * slope).astype(BF16)
    terms[...] = jnp.zeros(terms.shape, F32)
    for ab in range(9):
        a, b = ab // 3, ab % 3
        for x in range(nx):
            part = jnp.dot(grad[x], wide[ab], preferred_element_type=F32)
            terms[x + a, b : b + ny] += part.reshape(ny, nz, 3 * width)
    for j in range(parts_n):
        spot = lax.bitwise_xor(mine, j) * py + 1
        value = terms[:, pl.ds(spot, py)]
        total = value[..., width : 2 * width]
        total = total + roll_z(value[..., :width], -1) + roll_z(value[..., 2 * width :], 1)
        sends[j][...] = total.reshape(nx + 2, py * nz, width).astype(sends[j].dtype)


def deep_grad_body(windows, grad, theirs, mine, held):
    nx, rows, filters = grad.shape
    width = windows.shape[3] // 3
    turned = grad[...].reshape(nx * rows, filters).astype(F32).T.astype(BF16)
    chips, step, _ = mine.shape
    part = filters // 2
    total = 27 * part
    if chips * step > total:
        held[:, total:] = jnp.zeros((2, chips * step - total, width), F32)
    for ab in range(9):
        a, b = ab // 3, ab % 3
        value = jnp.dot(
            turned,
            windows[b, a : a + nx].reshape(nx * rows, 3 * width),
            preferred_element_type=F32,
        )
        for c in range(3):
            spot = (3 * ab + c) * part
            for side in range(2):
                held[side, spot : spot + part] = value[
                    side * part : (side + 1) * part, c * width : (c + 1) * width
                ]
    core = lax.rem(lax.axis_index("space"), 2)
    for q in range(chips):
        theirs[q] = held[1 - core, q * step : (q + 1) * step].astype(theirs.dtype)
        mine[q] = held[core, q * step : (q + 1) * step]


def early_grad_body(nz, *refs):
    parts, (sg, turned, deep, out, grad, held) = refs[:-6], refs[-6:]
    ext, rows, wide = sg.shape
    total = parts[0][...]
    for part in parts[1:]:
        total = total + part[...].astype(F32)
    px, prow, _ = total.shape
    py = prow // nz
    total = jnp.concatenate([total, total], axis=2).reshape(px, py, 1, nz, wide)
    total = jnp.broadcast_to(total, (px, py, 2, nz, wide)).reshape(px, rows, wide)
    for x in range(ext):
        grad[x] = (total[x // 2] * sg[x]).astype(BF16)
    early_grad_half(1 - lax.rem(lax.axis_index("space"), 2), grad, turned, deep, out, held)


def early_grad_rest_body(grad, turned, deep, out, held):
    early_grad_half(lax.rem(lax.axis_index("space"), 2), grad, turned, deep, out, held)


def early_grad_half(side, grad, turned, deep, out, held):
    ext, rows, wide = grad.shape
    width = wide // 2
    part = turned.shape[2] // 4
    right = grad[...].reshape(ext * rows, wide)
    for ab in range(9):
        a, b = ab // 3, ab % 3
        value = jnp.dot(
            turned[b, side, :, a * rows : (a + ext) * rows], right, preferred_element_type=F32
        )
        for c in range(3):
            spot = (3 * ab + c) * part
            held[spot : spot + part] = (
                value[c * part : (c + 1) * part, :width]
                + value[(c + 1) * part : (c + 2) * part, width:]
            )
    step = held.shape[0] // out.shape[0]
    for q in range(out.shape[0]):
        out[q, :step] = held[q * step : (q + 1) * step].astype(out.dtype)
        out[q, step:] = deep[q].astype(out.dtype)


def core_sum_body(mine, other, *outs):
    chip = lax.div(lax.axis_index("space"), 2)
    for j, out in enumerate(outs):
        q = lax.bitwise_xor(chip, j)
        out[...] = (mine[q] + other[q].astype(F32)).astype(out.dtype)


def chip_sum_body(count, step, *refs):
    others, (deep, *outs, held) = refs[:count], refs[count:]
    total = others[0][...]
    for ref in others[1:]:
        total = total + ref[...].astype(F32)
    held[:step] = total[:step]
    if held.shape[0] > step:
        held[step:] = jnp.zeros((held.shape[0] - step, total.shape[1]), F32)
    deep[...] = total[step:].astype(BF16)
    size = outs[0].shape[0]
    for j, out in enumerate(outs):
        spot = pl.multiple_of(lax.bitwise_xor(lax.axis_index("filt"), j) * size, 8)
        out[...] = held[pl.ds(spot, size)].astype(out.dtype)


def sum_body(*refs):
    total = refs[0][...]
    for ref in refs[1:-1]:
        total = total + ref[...].astype(F32)
    refs[-1][...] = total.astype(BF16)


def line_up_body(*refs):
    shares, deep, out = refs[:-2], refs[-2], refs[-1]
    size = shares[0].shape[0]
    for j, share in enumerate(shares):
        spot = pl.multiple_of(lax.bitwise_xor(lax.axis_index("filt"), j) * size, 16)
        out[pl.ds(spot, size)] = share[...]
    out[size * len(shares) :] = deep[...]


def stack_body(*refs):
    out = refs[-1]
    chip = lax.div(lax.axis_index("space"), 2)
    for j, ref in enumerate(refs[:-1]):
        out[lax.bitwise_xor(chip, j)] = ref[...]


def finish_body(own, early_scale, deep_scale, early_rows, deep_rows, pieces, *refs):
    early, deep, early_held, deep_held, sem = refs[-5:]
    core = lax.rem(lax.axis_index("space"), 2)
    side = core if own else 1 - core
    copies = []
    for out, held, first, step, scale in (
        (early, early_held, 0, early_rows, early_scale),
        (deep, deep_held, pieces.shape[1] - deep_rows, deep_rows, deep_scale),
    ):
        part = held.shape[1]
        for tap in range(27):
            row = tap * part
            while row < (tap + 1) * part:
                q, inner = row // step, row % step
                size = min(step - inner, (tap + 1) * part - row)
                spot = row - tap * part
                held[tap, spot : spot + size] = (
                    pieces[q, first + inner : first + inner + size].astype(F32) * scale
                )
                row += size
            if tap % 9 == 8:
                taps = pl.ds(tap - 8, 9)
                copy = pltpu.make_async_copy(
                    held.at[taps], out.at[taps, pl.ds(side * part, part)], sem.at[len(copies)]
                )
                copy.start()
                copies.append(copy)
    for copy in copies:
        copy.wait()


def paired(values, axis, step=1):
    count = lax.axis_size(axis)
    got = {
        j: lax.ppermute(values[j], axis, [(i, i ^ (step * j)) for i in range(count)])
        for j in reversed(range(1, len(values)))
    }
    return [values[0]] + [got[j] for j in range(1, len(values))]


def backward(values):
    return [values[0]] + values[:0:-1]


def both_sides(low, high, axis):
    count = lax.axis_size(axis)
    forward = [(i, i + 1) for i in range(count - 1)]
    backward = [(i + 1, i) for i in range(count - 1)]
    return lax.ppermute(high, axis, forward), lax.ppermute(low, axis, backward)


def shards(volume, w_early, w_deep, cotangent):
    nx, ny, nz, cin = volume.shape
    width = w_early.shape[2]
    filters = w_deep.shape[2]
    space = lax.axis_size("space")
    filt = lax.axis_size("filt")
    chips = space // 2
    half = nz // 2
    ext = nx + 6
    rows = ny * half
    ylo, yhi = both_sides(volume[:, :1], volume[:, ny - 1 :], "filt")
    xlo, xhi = both_sides(volume, volume, "space")
    sides = call(
        sides_body,
        "sides",
        struct((nx, 2, nz, cin)),
        (ylo, yhi),
        flops=1 << 32,
        moved=1 << 24,
    )
    clo, chi = both_sides(sides, sides, "space")
    windows, sg, pooled = call(
        early_body,
        "early_conv",
        (
            struct((3, ext, rows, 4 * cin)),
            struct((nx + 4, rows, 2 * width), F32),
            struct((nx // 2 + 2, rows // 2, width)),
        ),
        (volume, xlo, xhi, ylo, yhi, clo, chi, w_early.reshape(9, 3, cin, width)),
        [
            pltpu.VMEM(volume.shape, BF16),
            pltpu.VMEM((ext, ny + 2, nz + 16, cin), F32),
            pltpu.VMEM((9, 4 * cin, 2 * width), BF16),
            DMA((1,)),
            DMA((3, 6)),
        ],
        flops=2 * (nx + 4) * rows * 36 * cin * 2 * width,
        hbm=(0, 7),
    )
    parts = paired([pooled] * filt, "filt")
    turned = call(
        transpose_body,
        "turn_windows",
        struct((3, 2, 2 * cin, ext * rows)),
        (windows,),
        flops=1 << 30,
    )
    *parts, turned = lax.optimization_barrier((*parts, turned))
    dx, dy, dz, _ = cotangent.shape
    px = dx + 2
    prow = rows // 2
    deep = call(
        functools.partial(deep_body, filt),
        "deep_conv",
        [
            struct(cotangent.shape),
            struct((dx, dy * dz, filters)),
            struct((3, px, dy * dz, 3 * width)),
            struct((px, prow, width), F32),
        ]
        + [struct((px, prow, width))] * (filt - 1),
        (*parts, jnp.swapaxes(w_deep, 1, 2).reshape(9, 3, filters, width), cotangent),
        [
            pltpu.VMEM((px, dy + 2, dz, width), F32),
            pltpu.VMEM((px, dy + 2, dz, 3 * width), F32),
            pltpu.VMEM((9, filters, 3 * width), BF16),
            pltpu.VMEM(cotangent.shape, BF16),
            DMA((4,)),
        ],
        hbm=(filt, filt + 1),
        flops=4 * dx * dy * dz * 27 * width * filters,
    )
    block_out, grad, deep_windows = deep[:3]
    terms = paired(deep[3:], "filt")

    early_rows = 27 * cin // space
    deep_rows = ceil_to(-(-27 * filters // space), 16)
    deep_first, deep_second = call(
        deep_grad_body,
        "deep_grad",
        [struct((chips, deep_rows, width)), struct((chips, deep_rows, width), F32)],
        (deep_windows, grad),
        [pltpu.VMEM((2, chips * deep_rows, width), F32)],
        flops=2 * dx * dy * dz * 27 * width * filters,
    )
    piece = (chips, early_rows + deep_rows, width)
    held = pltpu.VMEM((27 * cin // 2, width), F32)
    flops = (nx + 4) * rows * 36 * cin * 2 * width
    theirs, grad = call(
        functools.partial(early_grad_body, half),
        "early_grad",
        [struct(piece), struct((nx + 4, rows, 2 * width))],
        (*backward(terms), sg, turned, deep_first),
        [held],
        flops=flops,
    )
    theirs = lax.ppermute(theirs, "space", [(i, i ^ 1) for i in range(space)])
    mine = call(
        early_grad_rest_body,
        "early_grad_rest",
        struct(piece, F32),
        (grad, turned, deep_second),
        [held],
        flops=flops,
    )
    sums = call(
        core_sum_body,
        "core_sum",
        [struct(piece[1:], F32)] + [struct(piece[1:])] * (chips - 1),
        (mine, theirs),
    )
    sums = backward(paired(sums, "space", 2))
    small = ceil_to(-(-early_rows // filt), 16)
    deep_sum, *shares = call(
        functools.partial(chip_sum_body, chips, early_rows),
        "chip_sum",
        [struct((deep_rows, width)), struct((small, width), F32)]
        + [struct((small, width))] * (filt - 1),
        sums,
        [pltpu.VMEM((small * filt, width), F32)],
    )
    share = call(sum_body, "filt_sum", struct((small, width)), backward(paired(shares, "filt")))
    shares = paired([share] * filt, "filt")
    final_rows = small * filt + deep_rows
    final = call(line_up_body, "line_up", struct((final_rows, width)), (*shares, deep_sum))
    finals = paired([final] * chips, "space", 2)
    own = call(stack_body, "stack", struct((chips, final_rows, width)), finals)
    other = lax.ppermute(own, "space", [(i, i ^ 1) for i in range(space)])
    early_total = nx * ny * nz * space * filt
    deep_total = dx * dy * dz * space
    results = [struct((27, cin, width), F32), struct((27, filters, width), F32)]
    scales = (1.0 / math.sqrt(early_total), 1.0 / math.sqrt(deep_total), early_rows, deep_rows)
    scratch = [
        pltpu.VMEM((27, cin // 2, width), F32),
        pltpu.VMEM((27, filters // 2, width), F32),
        DMA((6,)),
    ]
    results = call(
        functools.partial(finish_body, True, *scales),
        "finish_own",
        results,
        (own,),
        scratch,
        outs=HBM,
    )
    grad_early, grad_deep = call(
        functools.partial(finish_body, False, *scales),
        "finish_other",
        [struct(value.shape, F32) for value in results],
        (other, *results),
        scratch,
        hbm=(1, 2),
        outs=HBM,
        alias=((1, 0), (2, 1)),
    )
    return (block_out, grad_early, jnp.swapaxes(grad_deep, 1, 2))


def solution(mesh):
    return jax.shard_map(
        shards,
        mesh=mesh,
        in_specs=(
            P("space", "filt", None, None),
            P(),
            P(None, None, "filt"),
            P("space", None, None, "filt"),
        ),
        out_specs=(P("space", None, None, "filt"), P(), P(None, None, "filt")),
        check_vma=False,
    )
```

profile of v0, /device:TPU:0, one launch (start us, length us, event | category | flops | bytes accessed | tf_op | source)
XLA Modules:
  0.0 89.3 jit_solution(6627288304270770400)
XLA Ops:
  0.6 0.7 fusion
  1.4 1.3 %collective-permute-start.3 = (bf16[4,1,16,128]{3,2,1,0:T(8,128)(2,1)S(1)}, bf16[4,1,16,128]{3,2,1,0:T(8,128)(2,1)S(1)}, u32[]{:S(2)}, u32[]{:S(2)}) collective-permute-start(bf16[4,1,16,128]{3,2,1,0:T(8,128)(2,1)S(1)} %get-tuple-element.67), channel_id=1, source_target_pairs={{1,0},{2,1},{3,2},{5,4},{6,5},{7,6},{9,8},{10,9},{11,10},{13,12},{... | collective-permute-start | bytes 49160 | tf_op jit(solution)/shard_map/ppermute | solution.py:370
  2.7 5.7 %collective-permute-start.2 = (bf16[4,1,16,128]{3,2,1,0:T(8,128)(2,1)S(1)}, bf16[4,1,16,128]{3,2,1,0:T(8,128)(2,1)S(1)}, u32[]{:S(2)}, u32[]{:S(2)}) collective-permute-start(bf16[4,1,16,128]{3,2,1,0:T(8,128)(2,1)S(1)} %get-tuple-element.68), channel_id=1, source_target_pairs={{0,1},{1,2},{2,3},{4,5},{5,6},{6,7},{8,9},{9,10},{10,11},{12,13},{... | collective-permute-start | bytes 49160 | tf_op jit(solution)/shard_map/ppermute | solution.py:370
  8.4 1.3 %collective-permute-start.1 = (bf16[4,16,16,128]{3,2,1,0:T(8,128)(2,1)}, bf16[4,16,16,128]{3,2,1,0:T(8,128)(2,1)S(1)}, u32[]{:S(2)}, u32[]{:S(2)}) collective-permute-start(bf16[4,16,16,128]{3,2,1,0:T(8,128)(2,1)} %volume.1), channel_id=1, source_target_pairs={{4,0},{8,4},{12,8},{16,12},{20,16},{24,20},{28,24},{5,1},{9,5},{13... | collective-permute-start | bytes 786440 | tf_op jit(solution)/shard_map/ppermute | solution.py:370
  9.7 3.1 %collective-permute-start = (bf16[4,16,16,128]{3,2,1,0:T(8,128)(2,1)}, bf16[4,16,16,128]{3,2,1,0:T(8,128)(2,1)S(1)}, u32[]{:S(2)}, u32[]{:S(2)}) collective-permute-start(bf16[4,16,16,128]{3,2,1,0:T(8,128)(2,1)} %volume.1), channel_id=1, source_target_pairs={{0,4},{4,8},{8,12},{12,16},{16,20},{20,24},{24,28},{1,5},{5,9},{9,... | collective-permute-start | bytes 786440 | tf_op jit(solution)/shard_map/ppermute | solution.py:370
  12.8 1.3 %collective-permute-start.5 = (bf16[4,2,16,128]{3,2,1,0:T(8,128)(2,1)S(1)}, bf16[4,2,16,128]{3,2,1,0:T(8,128)(2,1)S(1)}, u32[]{:S(2)}, u32[]{:S(2)}) collective-permute-start(bf16[4,2,16,128]{3,2,1,0:T(8,128)(2,1)S(1)} %sides.1), channel_id=1, source_target_pairs={{4,0},{8,4},{12,8},{16,12},{20,16},{24,20},{28,24},{5,1},{9,5},{13... | collective-permute-start | bytes 98312 | tf_op jit(solution)/shard_map/ppermute | solution.py:370
  14.1 4.1 %collective-permute-start.4 = (bf16[4,2,16,128]{3,2,1,0:T(8,128)(2,1)S(1)}, bf16[4,2,16,128]{3,2,1,0:T(8,128)(2,1)S(1)}, u32[]{:S(2)}, u32[]{:S(2)}) collective-permute-start(bf16[4,2,16,128]{3,2,1,0:T(8,128)(2,1)S(1)} %sides.1), channel_id=1, source_target_pairs={{0,4},{4,8},{8,12},{12,16},{16,20},{20,24},{24,28},{1,5},{5,9},{9,... | collective-permute-start | bytes 98312 | tf_op jit(solution)/shard_map/ppermute | solution.py:370
  18.2 0.8 collective-permute-done.4.clo
  19.0 5.0 %early_conv.1 = (bf16[3,10,128,512]{3,2,1,0:T(8,128)(2,1)S(1)}, f32[8,128,256]{2,1,0:T(8,128)S(1)}, bf16[4,64,128]{2,1,0:T(8,128)(2,1)S(1)}) custom-call(bf16[4,16,16,128]{3,2,1,0:T(8,128)(2,1)S(1)} %copy-done, bf16[4,16,16,128]{3,2,1,0:T(8,128)(2,1)S(1)} %collective-permute-done.xlo, bf16[4,16,16,128]{3,2,1,0:T(8,128)(2,1)S(1)} %collective-permute-done.1.xhi, ...), custom_call_target="tpu_custom_call" | custom-call | flops 2415919104 | bytes 1048576 | tf_op jit(solution)/shard_map/early_conv/pallas_call | solution.py:22
  24.0 1.5 %collective-permute-start.8 = (bf16[4,64,128]{2,1,0:T(8,128)(2,1)S(1)}, bf16[4,64,128]{2,1,0:T(8,128)(2,1)S(1)}, u32[]{:S(2)}, u32[]{:S(2)}) collective-permute-start(bf16[4,64,128]{2,1,0:T(8,128)(2,1)S(1)} %get-tuple-element.37.refs_0_), channel_id=1, source_target_pairs={{0,3},{1,2},{2,1},{3,0},{4,7},{5,6},{6,5},{7,4},{8,11},{9,10},{10,... | collective-permute-start | bytes 196616 | tf_op jit(solution)/shard_map/ppermute | solution.py:356
  25.4 1.6 %collective-permute-start.7 = (bf16[4,64,128]{2,1,0:T(8,128)(2,1)S(1)}, bf16[4,64,128]{2,1,0:T(8,128)(2,1)S(1)}, u32[]{:S(2)}, u32[]{:S(2)}) collective-permute-start(bf16[4,64,128]{2,1,0:T(8,128)(2,1)S(1)} %get-tuple-element.37.refs_0_), channel_id=1, source_target_pairs={{0,2},{1,3},{2,0},{3,1},{4,6},{5,7},{6,4},{7,5},{8,10},{9,11},{10,... | collective-permute-start | bytes 196616 | tf_op jit(solution)/shard_map/ppermute | solution.py:356
  27.1 1.3 %collective-permute-start.6 = (bf16[4,64,128]{2,1,0:T(8,128)(2,1)S(1)}, bf16[4,64,128]{2,1,0:T(8,128)(2,1)S(1)}, u32[]{:S(2)}, u32[]{:S(2)}) collective-permute-start(bf16[4,64,128]{2,1,0:T(8,128)(2,1)S(1)} %get-tuple-element.37.refs_0_), channel_id=1, source_target_pairs={{0,1},{1,0},{2,3},{3,2},{4,5},{5,4},{6,7},{7,6},{8,9},{9,8},{10,11... | collective-permute-start | bytes 196616 | tf_op jit(solution)/shard_map/ppermute | solution.py:356
  28.4 1.1 %turn_windows.1.refs_5_.turned = bf16[3,2,256,1280]{3,2,1,0:T(8,128)(2,1)S(1)} custom-call(bf16[3,10,128,512]{3,2,1,0:T(8,128)(2,1)S(1)} %get-tuple-element.36.windows), custom_call_target="tpu_custom_call" | custom-call | flops 1073741824 | bytes 1048576 | tf_op jit(solution)/shard_map/turn_windows/pallas_call | solution.py:22
  29.5 0.7 collective-permute-done.8.refs_3_
  30.2 3.5 %collective-permute-done.7.refs_2_ = bf16[4,64,128]{2,1,0:T(8,128)(2,1)S(1)} collective-permute-done((bf16[4,64,128]{2,1,0:T(8,128)(2,1)S(1)}, bf16[4,64,128]{2,1,0:T(8,128)(2,1)S(1)}, u32[]{:S(2)}, u32[]{:S(2)}) %collective-permute-start.7) | collective-permute-done | bytes 65568 | tf_op jit(solution)/shard_map/ppermute | solution.py:356
  33.7 3.7 %deep_conv.1 = (bf16[2,32,8,64]{3,2,1,0:T(8,128)(2,1)}, bf16[2,256,64]{2,1,0:T(8,128)(2,1)S(1)}, bf16[3,4,256,384]{3,2,1,0:T(8,128)(2,1)S(1)}, f32[4,64,128]{2,1...) custom-call(bf16[4,64,128]{2,1,0:T(8,128)(2,1)S(1)} %get-tuple-eleme, ...), custom_call_target="tpu_custom_call" | custom-call | flops 452984832 | bytes 1048576 | tf_op jit(solution)/shard_map/deep_conv/pallas_call | solution.py:22
  37.4 2.6 %collective-permute-start.9 = (bf16[4,64,128]{2,1,0:T(8,128)(2,1)S(1)}, bf16[4,64,128]{2,1,0:T(8,128)(2,1)S(1)}, u32[]{:S(2)}, u32[]{:S(2)}) collective-permute-start(bf16[4,64,128]{2,1,0:T(8,128)(2,1)S(1)} %get-tuple-element.43), channel_id=1, source_target_pairs={{0,3},{1,2},{2,1},{3,0},{4,7},{5,6},{6,5},{7,4},{8,11},{9,10},{10,... | collective-permute-start | bytes 196616 | tf_op jit(solution)/shard_map/ppermute | solution.py:356
  40.0 1.9 %collective-permute-start.11 = (bf16[4,64,128]{2,1,0:T(8,128)(2,1)S(1)}, bf16[4,64,128]{2,1,0:T(8,128)(2,1)S(1)}, u32[]{:S(2)}, u32[]{:S(2)}) collective-permute-start(bf16[4,64,128]{2,1,0:T(8,128)(2,1)S(1)} %get-tuple-element.45), channel_id=1, source_target_pairs={{0,1},{1,0},{2,3},{3,2},{4,5},{5,4},{6,7},{7,6},{8,9},{9,8},{10,11... | collective-permute-start | bytes 196616 | tf_op jit(solution)/shard_map/ppermute | solution.py:356
  41.8 0.7 deep_grad.1
  42.6 1.6 %collective-permute-done.9.refs_1_ = bf16[4,64,128]{2,1,0:T(8,128)(2,1)S(1)} collective-permute-done((bf16[4,64,128]{2,1,0:T(8,128)(2,1)S(1)}, bf16[4,64,128]{2,1,0:T(8,128)(2,1)S(1)}, u32[]{:S(2)}, u32[]{:S(2)}) %collective-permute-start.9) | collective-permute-done | bytes 65568 | tf_op jit(solution)/shard_map/ppermute | solution.py:356
  44.2 2.3 %collective-permute-done.10.refs_2_ = bf16[4,64,128]{2,1,0:T(8,128)(2,1)S(1)} collective-permute-done((bf16[4,64,128]{2,1,0:T(8,128)(2,1)S(1)}, bf16[4,64,128]{2,1,0:T(8,128)(2,1)S(1)}, u32[]{:S(2)}, u32[]{:S(2)}) %collective-permute-start.10) | collective-permute-done | bytes 65568 | tf_op jit(solution)/shard_map/ppermute | solution.py:356
  46.5 1.4 %early_grad.1 = (bf16[4,656,128]{2,1,0:T(8,128)(2,1)S(1)}, bf16[8,128,256]{2,1,0:T(8,128)(2,1)S(1)}) custom-call(f32[4,64,128]{2,1,0:T(8,128)S(1)} %get-tuple-element.42.refs_0_, bf16[4,64,128]{2,1,0:T(8,128)(2,1)S(1)} %collective-permute-done.9.refs_1_, bf16[4,64,128]{2,1,0:T(8,128)(2,1)S(1)} %collective-permute-done.10.refs_2_, ...), custom_call_target="tpu_custom_call" | custom-call | flops 1207959552 | bytes 1048576 | tf_op jit(solution)/shard_map/early_grad/pallas_call | solution.py:22
  48.1 1.4 %early_grad_rest.1.mine = f32[4,656,128]{2,1,0:T(8,128)S(1)} custom-call(bf16[8,128,256]{2,1,0:T(8,128)(2,1)S(1)} %get-tuple-element.51.grad, bf16[3,2,256,1280]{3,2,1,0:T(8,128)(2,1)S(1)} %turn_windows.1.refs_5_.turned, f32[4,224,128]{2,1,0:T(8,128)S(1)} %get-tuple-element.52.deep), custom_call_target="tpu_custom_call" | custom-call | flops 1207959552 | bytes 1048576 | tf_op jit(solution)/shard_map/early_grad_rest/pallas_call | solution.py:22
  49.4 0.7 collective-permute-done.12.other
  50.2 0.1 core_sum.1
  50.3 1.8 %collective-permute-start.13 = (bf16[656,128]{1,0:T(8,128)(2,1)S(1)}, bf16[656,128]{1,0:T(8,128)(2,1)S(1)}, u32[]{:S(2)}, u32[]{:S(2)}) collective-permute-start(bf16[656,128]{1,0:T(8,128)(2,1)S(1)} %get-tuple-element.55), channel_id=1, source_target_pairs={{0,24},{4,28},{8,16},{12,20},{16,8},{20,12},{24,0},{28,4},{1,25},{... | collective-permute-start | bytes 503816 | tf_op jit(solution)/shard_map/ppermute | solution.py:356
  52.1 3.2 %collective-permute-start.14 = (bf16[656,128]{1,0:T(8,128)(2,1)S(1)}, bf16[656,128]{1,0:T(8,128)(2,1)S(1)}, u32[]{:S(2)}, u32[]{:S(2)}) collective-permute-start(bf16[656,128]{1,0:T(8,128)(2,1)S(1)} %get-tuple-element.56), channel_id=1, source_target_pairs={{0,16},{4,20},{8,24},{12,28},{16,0},{20,4},{24,8},{28,12},{1,17},{... | collective-permute-start | bytes 503816 | tf_op jit(solution)/shard_map/ppermute | solution.py:356
  55.3 2.6 %collective-permute-done.13.refs_1_ = bf16[656,128]{1,0:T(8,128)(2,1)S(1)} collective-permute-done((bf16[656,128]{1,0:T(8,128)(2,1)S(1)}, bf16[656,128]{1,0:T(8,128)(2,1)S(1)}, u32[]{:S(2)}, u32[]{:S(2)}) %collective-permute-start.13) | collective-permute-done | bytes 167968 | tf_op jit(solution)/shard_map/ppermute | solution.py:356
  57.9 3.9 %collective-permute-done.14.refs_2_ = bf16[656,128]{1,0:T(8,128)(2,1)S(1)} collective-permute-done((bf16[656,128]{1,0:T(8,128)(2,1)S(1)}, bf16[656,128]{1,0:T(8,128)(2,1)S(1)}, u32[]{:S(2)}, u32[]{:S(2)}) %collective-permute-start.14) | collective-permute-done | bytes 167968 | tf_op jit(solution)/shard_map/ppermute | solution.py:356
  61.8 1.1 %collective-permute-done.15.refs_3_ = bf16[656,128]{1,0:T(8,128)(2,1)S(1)} collective-permute-done((bf16[656,128]{1,0:T(8,128)(2,1)S(1)}, bf16[656,128]{1,0:T(8,128)(2,1)S(1)}, u32[]{:S(2)}, u32[]{:S(2)}) %collective-permute-start.15) | collective-permute-done | bytes 167968 | tf_op jit(solution)/shard_map/ppermute | solution.py:356
  63.0 2.4 %collective-permute-start.16 = (bf16[112,128]{1,0:T(8,128)(2,1)S(1)}, bf16[112,128]{1,0:T(8,128)(2,1)S(1)}, u32[]{:S(2)}, u32[]{:S(2)}) collective-permute-start(bf16[112,128]{1,0:T(8,128)(2,1)S(1)} %get-tuple-element.59), channel_id=1, source_target_pairs={{0,3},{1,2},{2,1},{3,0},{4,7},{5,6},{6,5},{7,4},{8,11},{9,10},{10,... | collective-permute-start | bytes 86024 | tf_op jit(solution)/shard_map/ppermute | solution.py:356
  65.4 2.1 %collective-permute-start.18 = (bf16[112,128]{1,0:T(8,128)(2,1)S(1)}, bf16[112,128]{1,0:T(8,128)(2,1)S(1)}, u32[]{:S(2)}, u32[]{:S(2)}) collective-permute-start(bf16[112,128]{1,0:T(8,128)(2,1)S(1)} %get-tuple-element.61), channel_id=1, source_target_pairs={{0,1},{1,0},{2,3},{3,2},{4,5},{5,4},{6,7},{7,6},{8,9},{9,8},{10,11... | collective-permute-start | bytes 86024 | tf_op jit(solution)/shard_map/ppermute | solution.py:356
  67.5 1.3 %collective-permute-done.16.refs_1_ = bf16[112,128]{1,0:T(8,128)(2,1)S(1)} collective-permute-done((bf16[112,128]{1,0:T(8,128)(2,1)S(1)}, bf16[112,128]{1,0:T(8,128)(2,1)S(1)}, u32[]{:S(2)}, u32[]{:S(2)}) %collective-permute-start.16) | collective-permute-done | bytes 28704 | tf_op jit(solution)/shard_map/ppermute | solution.py:356
  68.7 1.4 %collective-permute-done.17.refs_2_ = bf16[112,128]{1,0:T(8,128)(2,1)S(1)} collective-permute-done((bf16[112,128]{1,0:T(8,128)(2,1)S(1)}, bf16[112,128]{1,0:T(8,128)(2,1)S(1)}, u32[]{:S(2)}, u32[]{:S(2)}) %collective-permute-start.17) | collective-permute-done | bytes 28704 | tf_op jit(solution)/shard_map/ppermute | solution.py:356
  70.2 2.0 %collective-permute-start.21 = (bf16[112,128]{1,0:T(8,128)(2,1)S(1)}, bf16[112,128]{1,0:T(8,128)(2,1)S(1)}, u32[]{:S(2)}, u32[]{:S(2)}) collective-permute-start(bf16[112,128]{1,0:T(8,128)(2,1)S(1)} %filt_sum.1.refs_0_), channel_id=1, source_target_pairs={{0,3},{1,2},{2,1},{3,0},{4,7},{5,6},{6,5},{7,4},{8,11},{9,10},{10,... | collective-permute-start | bytes 86024 | tf_op jit(solution)/shard_map/ppermute | solution.py:356
  72.2 0.7 collective-permute-start.20
  72.9 1.8 %collective-permute-start.19 = (bf16[112,128]{1,0:T(8,128)(2,1)S(1)}, bf16[112,128]{1,0:T(8,128)(2,1)S(1)}, u32[]{:S(2)}, u32[]{:S(2)}) collective-permute-start(bf16[112,128]{1,0:T(8,128)(2,1)S(1)} %filt_sum.1.refs_0_), channel_id=1, source_target_pairs={{0,1},{1,0},{2,3},{3,2},{4,5},{5,4},{6,7},{7,6},{8,9},{9,8},{10,11... | collective-permute-start | bytes 86024 | tf_op jit(solution)/shard_map/ppermute | solution.py:356
  74.7 1.3 %collective-permute-done.21.refs_3_ = bf16[112,128]{1,0:T(8,128)(2,1)S(1)} collective-permute-done((bf16[112,128]{1,0:T(8,128)(2,1)S(1)}, bf16[112,128]{1,0:T(8,128)(2,1)S(1)}, u32[]{:S(2)}, u32[]{:S(2)}) %collective-permute-start.21) | collective-permute-done | bytes 28704 | tf_op jit(solution)/shard_map/ppermute | solution.py:356
  75.9 1.4 %collective-permute-done.20.refs_2_ = bf16[112,128]{1,0:T(8,128)(2,1)S(1)} collective-permute-done((bf16[112,128]{1,0:T(8,128)(2,1)S(1)}, bf16[112,128]{1,0:T(8,128)(2,1)S(1)}, u32[]{:S(2)}, u32[]{:S(2)}) %collective-permute-start.20) | collective-permute-done | bytes 28704 | tf_op jit(solution)/shard_map/ppermute | solution.py:356
  77.3 1.7 %collective-permute-start.24 = (bf16[672,128]{1,0:T(8,128)(2,1)S(1)}, bf16[672,128]{1,0:T(8,128)(2,1)S(1)}, u32[]{:S(2)}, u32[]{:S(2)}) collective-permute-start(bf16[672,128]{1,0:T(8,128)(2,1)S(1)} %line_up.1.refs_0_), channel_id=1, source_target_pairs={{0,24},{4,28},{8,16},{12,20},{16,8},{20,12},{24,0},{28,4},{1,25},{... | collective-permute-start | bytes 516104 | tf_op jit(solution)/shard_map/ppermute | solution.py:356
  79.0 1.3 %collective-permute-start.23 = (bf16[672,128]{1,0:T(8,128)(2,1)S(1)}, bf16[672,128]{1,0:T(8,128)(2,1)S(1)}, u32[]{:S(2)}, u32[]{:S(2)}) collective-permute-start(bf16[672,128]{1,0:T(8,128)(2,1)S(1)} %line_up.1.refs_0_), channel_id=1, source_target_pairs={{0,16},{4,20},{8,24},{12,28},{16,0},{20,4},{24,8},{28,12},{1,17},{... | collective-permute-start | bytes 516104 | tf_op jit(solution)/shard_map/ppermute | solution.py:356
  80.3 0.6 collective-permute-start.22
  80.9 2.9 %collective-permute-done.24.refs_3_ = bf16[672,128]{1,0:T(8,128)(2,1)S(1)} collective-permute-done((bf16[672,128]{1,0:T(8,128)(2,1)S(1)}, bf16[672,128]{1,0:T(8,128)(2,1)S(1)}, u32[]{:S(2)}, u32[]{:S(2)}) %collective-permute-start.24) | collective-permute-done | bytes 172064 | tf_op jit(solution)/shard_map/ppermute | solution.py:356
  83.8 1.7 %collective-permute-done.23.refs_2_ = bf16[672,128]{1,0:T(8,128)(2,1)S(1)} collective-permute-done((bf16[672,128]{1,0:T(8,128)(2,1)S(1)}, bf16[672,128]{1,0:T(8,128)(2,1)S(1)}, u32[]{:S(2)}, u32[]{:S(2)}) %collective-permute-start.23) | collective-permute-done | bytes 172064 | tf_op jit(solution)/shard_map/ppermute | solution.py:356
  85.5 0.2 collective-permute-done.22.refs_1_
  85.9 1.1 %finish_own.1 = (f32[27,128,128]{2,1,0:T(8,128)}, f32[27,64,128]{2,1,0:T(8,128)}) custom-call(bf16[4,672,128]{2,1,0:T(8,128)(2,1)S(1)} %stack.1.pieces), custom_call_target="tpu_custom_call" | custom-call | bytes 1048576 | tf_op jit(solution)/shard_map/finish_own/pallas_call | solution.py:22
  87.0 1.0 %collective-permute-done.25.pieces = bf16[4,672,128]{2,1,0:T(8,128)(2,1)S(1)} collective-permute-done((bf16[4,672,128]{2,1,0:T(8,128)(2,1)S(1)}, bf16[4,672,128]{2,1,0:T(8,128)(2,1)S(1)}, u32[]{:S(2)}, u32[]{:S(2)}) %collective-permute-start.25) | collective-permute-done | bytes 688160 | tf_op jit(solution)/shard_map/ppermute | solution.py:501
  88.0 1.1 %finish_other.1 = (f32[27,128,128]{2,1,0:T(8,128)}, f32[27,64,128]{2,1,0:T(8,128)}) custom-call(bf16[4,672,128]{2,1,0:T(8,128)(2,1)S(1)} %collective-permute-done.25.pieces, f32[27,128,128]{2,1,0:T(8,128)} %get-tuple-element.63.refs_0_, f32[27,64,128]{2,1,0:T(8,128)} %get-tuple-element.64.refs_1_), custom_call_target="tpu_custom_call", output_to_operand_aliasing={{0}: (1, {}), {1}: (2, {})} | custom-call | bytes 1048576 | tf_op jit(solution)/shard_map/finish_other/pallas_call | solution.py:22
  (27 shorter events, 0.4 us)
Async XLA Ops:
  1.4 11.4 %collective-permute-start.3 = (bf16[4,1,16,128]{3,2,1,0:T(8,128)(2,1)S(1)}, bf16[4,1,16,128]{3,2,1,0:T(8,128)(2,1)S(1)}, u32[]{:S(2)}, u32[]{:S(2)}) collective-permute-start(bf16[4,1,16,128]{3,2,1,0:T(8,128)(2,1)S(1)} %get-tuple-element.67), channel_id=1, source_target_pairs={{1,0},{2,1},{3,2},{5,4},{6,5},{7,6},{9,8},{10,9},{11,10},{13,12},{... | collective-permute-start | bytes 49160 | tf_op jit(solution)/shard_map/ppermute | solution.py:370
  2.7 16.3 %copy-start = (bf16[4,16,16,128]{3,2,1,0:T(8,128)(2,1)S(1)}, bf16[4,16,16,128]{3,2,1,0:T(8,128)(2,1)}, u32[]{:S(2)}) copy-start(bf16[4,16,16,128]{3,2,1,0:T(8,128)(2,1)} %volume.1) | copy-start | bytes 786436
  2.7 16.3 %copy-start.1 = (bf16[27,128,128]{2,1,0:T(8,128)(2,1)S(1)}, bf16[27,128,128]{2,1,0:T(8,128)(2,1)}, u32[]{:S(2)}) copy-start(bf16[27,128,128]{2,1,0:T(8,128)(2,1)} %param.5) | copy-start | bytes 2654212
  2.7 10.1 %collective-permute-start.2 = (bf16[4,1,16,128]{3,2,1,0:T(8,128)(2,1)S(1)}, bf16[4,1,16,128]{3,2,1,0:T(8,128)(2,1)S(1)}, u32[]{:S(2)}, u32[]{:S(2)}) collective-permute-start(bf16[4,1,16,128]{3,2,1,0:T(8,128)(2,1)S(1)} %get-tuple-element.68), channel_id=1, source_target_pairs={{0,1},{1,2},{2,3},{4,5},{5,6},{6,7},{8,9},{9,10},{10,11},{12,13},{... | collective-permute-start | bytes 49160 | tf_op jit(solution)/shard_map/ppermute | solution.py:370
  8.4 10.6 %collective-permute-start.1 = (bf16[4,16,16,128]{3,2,1,0:T(8,128)(2,1)}, bf16[4,16,16,128]{3,2,1,0:T(8,128)(2,1)S(1)}, u32[]{:S(2)}, u32[]{:S(2)}) collective-permute-start(bf16[4,16,16,128]{3,2,1,0:T(8,128)(2,1)} %volume.1), channel_id=1, source_target_pairs={{4,0},{8,4},{12,8},{16,12},{20,16},{24,20},{28,24},{5,1},{9,5},{13... | collective-permute-start | bytes 786440 | tf_op jit(solution)/shard_map/ppermute | solution.py:370
  9.7 9.3 %collective-permute-start = (bf16[4,16,16,128]{3,2,1,0:T(8,128)(2,1)}, bf16[4,16,16,128]{3,2,1,0:T(8,128)(2,1)S(1)}, u32[]{:S(2)}, u32[]{:S(2)}) collective-permute-start(bf16[4,16,16,128]{3,2,1,0:T(8,128)(2,1)} %volume.1), channel_id=1, source_target_pairs={{0,4},{4,8},{8,12},{12,16},{16,20},{20,24},{24,28},{1,5},{5,9},{9,... | collective-permute-start | bytes 786440 | tf_op jit(solution)/shard_map/ppermute | solution.py:370
  12.8 5.4 %collective-permute-start.5 = (bf16[4,2,16,128]{3,2,1,0:T(8,128)(2,1)S(1)}, bf16[4,2,16,128]{3,2,1,0:T(8,128)(2,1)S(1)}, u32[]{:S(2)}, u32[]{:S(2)}) collective-permute-start(bf16[4,2,16,128]{3,2,1,0:T(8,128)(2,1)S(1)} %sides.1), channel_id=1, source_target_pairs={{4,0},{8,4},{12,8},{16,12},{20,16},{24,20},{28,24},{5,1},{9,5},{13... | collective-permute-start | bytes 98312 | tf_op jit(solution)/shard_map/ppermute | solution.py:370
  14.1 4.9 %collective-permute-start.4 = (bf16[4,2,16,128]{3,2,1,0:T(8,128)(2,1)S(1)}, bf16[4,2,16,128]{3,2,1,0:T(8,128)(2,1)S(1)}, u32[]{:S(2)}, u32[]{:S(2)}) collective-permute-start(bf16[4,2,16,128]{3,2,1,0:T(8,128)(2,1)S(1)} %sides.1), channel_id=1, source_target_pairs={{0,4},{4,8},{8,12},{12,16},{16,20},{20,24},{24,28},{1,5},{5,9},{9,... | collective-permute-start | bytes 98312 | tf_op jit(solution)/shard_map/ppermute | solution.py:370
  24.0 6.2 %collective-permute-start.8 = (bf16[4,64,128]{2,1,0:T(8,128)(2,1)S(1)}, bf16[4,64,128]{2,1,0:T(8,128)(2,1)S(1)}, u32[]{:S(2)}, u32[]{:S(2)}) collective-permute-start(bf16[4,64,128]{2,1,0:T(8,128)(2,1)S(1)} %get-tuple-element.37.refs_0_), channel_id=1, source_target_pairs={{0,3},{1,2},{2,1},{3,0},{4,7},{5,6},{6,5},{7,4},{8,11},{9,10},{10,... | collective-permute-start | bytes 196616 | tf_op jit(solution)/shard_map/ppermute | solution.py:356
  25.4 8.2 %collective-permute-start.7 = (bf16[4,64,128]{2,1,0:T(8,128)(2,1)S(1)}, bf16[4,64,128]{2,1,0:T(8,128)(2,1)S(1)}, u32[]{:S(2)}, u32[]{:S(2)}) collective-permute-start(bf16[4,64,128]{2,1,0:T(8,128)(2,1)S(1)} %get-tuple-element.37.refs_0_), channel_id=1, source_target_pairs={{0,2},{1,3},{2,0},{3,1},{4,6},{5,7},{6,4},{7,5},{8,10},{9,11},{10,... | collective-permute-start | bytes 196616 | tf_op jit(solution)/shard_map/ppermute | solution.py:356
  27.1 6.6 %collective-permute-start.6 = (bf16[4,64,128]{2,1,0:T(8,128)(2,1)S(1)}, bf16[4,64,128]{2,1,0:T(8,128)(2,1)S(1)}, u32[]{:S(2)}, u32[]{:S(2)}) collective-permute-start(bf16[4,64,128]{2,1,0:T(8,128)(2,1)S(1)} %get-tuple-element.37.refs_0_), channel_id=1, source_target_pairs={{0,1},{1,0},{2,3},{3,2},{4,5},{5,4},{6,7},{7,6},{8,9},{9,8},{10,11... | collective-permute-start | bytes 196616 | tf_op jit(solution)/shard_map/ppermute | solution.py:356
  28.4 5.2 %copy-start.2 = (bf16[27,128,64]{1,2,0:T(8,128)(2,1)S(1)}, bf16[27,128,64]{1,2,0:T(8,128)(2,1)}, u32[]{:S(2)}) copy-start(bf16[27,128,64]{1,2,0:T(8,128)(2,1)} %param.6) | copy-start | bytes 1327108
  28.4 5.2 %copy-start.3 = (bf16[2,32,8,64]{3,2,1,0:T(8,128)(2,1)S(1)}, bf16[2,32,8,64]{3,2,1,0:T(8,128)(2,1)}, u32[]{:S(2)}) copy-start(bf16[2,32,8,64]{3,2,1,0:T(8,128)(2,1)} %refs_5_.1) | copy-start | bytes 196612
  37.4 6.8 %collective-permute-start.9 = (bf16[4,64,128]{2,1,0:T(8,128)(2,1)S(1)}, bf16[4,64,128]{2,1,0:T(8,128)(2,1)S(1)}, u32[]{:S(2)}, u32[]{:S(2)}) collective-permute-start(bf16[4,64,128]{2,1,0:T(8,128)(2,1)S(1)} %get-tuple-element.43), channel_id=1, source_target_pairs={{0,3},{1,2},{2,1},{3,0},{4,7},{5,6},{6,5},{7,4},{8,11},{9,10},{10,... | collective-permute-start | bytes 196616 | tf_op jit(solution)/shard_map/ppermute | solution.py:356
  40.0 6.6 %collective-permute-start.10 = (bf16[4,64,128]{2,1,0:T(8,128)(2,1)S(1)}, bf16[4,64,128]{2,1,0:T(8,128)(2,1)S(1)}, u32[]{:S(2)}, u32[]{:S(2)}) collective-permute-start(bf16[4,64,128]{2,1,0:T(8,128)(2,1)S(1)} %get-tuple-element.44), channel_id=1, source_target_pairs={{0,2},{1,3},{2,0},{3,1},{4,6},{5,7},{6,4},{7,5},{8,10},{9,11},{10,... | collective-permute-start | bytes 196616 | tf_op jit(solution)/shard_map/ppermute | solution.py:356
  40.0 6.6 %collective-permute-start.11 = (bf16[4,64,128]{2,1,0:T(8,128)(2,1)S(1)}, bf16[4,64,128]{2,1,0:T(8,128)(2,1)S(1)}, u32[]{:S(2)}, u32[]{:S(2)}) collective-permute-start(bf16[4,64,128]{2,1,0:T(8,128)(2,1)S(1)} %get-tuple-element.45), channel_id=1, source_target_pairs={{0,1},{1,0},{2,3},{3,2},{4,5},{5,4},{6,7},{7,6},{8,9},{9,8},{10,11... | collective-permute-start | bytes 196616 | tf_op jit(solution)/shard_map/ppermute | solution.py:356
  48.0 2.2 %collective-permute-start.12 = (bf16[4,656,128]{2,1,0:T(8,128)(2,1)S(1)}, bf16[4,656,128]{2,1,0:T(8,128)(2,1)S(1)}, u32[]{:S(2)}, u32[]{:S(2)}) collective-permute-start(bf16[4,656,128]{2,1,0:T(8,128)(2,1)S(1)} %get-tuple-element.53), channel_id=1, source_target_pairs={{0,4},{4,0},{8,12},{12,8},{16,20},{20,16},{24,28},{28,24},{1,5},{5... | collective-permute-start | bytes 2015240 | tf_op jit(solution)/shard_map/ppermute | solution.py:470
  50.3 7.6 %collective-permute-start.13 = (bf16[656,128]{1,0:T(8,128)(2,1)S(1)}, bf16[656,128]{1,0:T(8,128)(2,1)S(1)}, u32[]{:S(2)}, u32[]{:S(2)}) collective-permute-start(bf16[656,128]{1,0:T(8,128)(2,1)S(1)} %get-tuple-element.55), channel_id=1, source_target_pairs={{0,24},{4,28},{8,16},{12,20},{16,8},{20,12},{24,0},{28,4},{1,25},{... | collective-permute-start | bytes 503816 | tf_op jit(solution)/shard_map/ppermute | solution.py:356
  52.1 9.7 %collective-permute-start.14 = (bf16[656,128]{1,0:T(8,128)(2,1)S(1)}, bf16[656,128]{1,0:T(8,128)(2,1)S(1)}, u32[]{:S(2)}, u32[]{:S(2)}) collective-permute-start(bf16[656,128]{1,0:T(8,128)(2,1)S(1)} %get-tuple-element.56), channel_id=1, source_target_pairs={{0,16},{4,20},{8,24},{12,28},{16,0},{20,4},{24,8},{28,12},{1,17},{... | collective-permute-start | bytes 503816 | tf_op jit(solution)/shard_map/ppermute | solution.py:356
  55.3 7.6 %collective-permute-start.15 = (bf16[656,128]{1,0:T(8,128)(2,1)S(1)}, bf16[656,128]{1,0:T(8,128)(2,1)S(1)}, u32[]{:S(2)}, u32[]{:S(2)}) collective-permute-start(bf16[656,128]{1,0:T(8,128)(2,1)S(1)} %get-tuple-element.57), channel_id=1, source_target_pairs={{0,8},{4,12},{8,0},{12,4},{16,24},{20,28},{24,16},{28,20},{1,9},{5... | collective-permute-start | bytes 503816 | tf_op jit(solution)/shard_map/ppermute | solution.py:356
  63.0 5.7 %collective-permute-start.16 = (bf16[112,128]{1,0:T(8,128)(2,1)S(1)}, bf16[112,128]{1,0:T(8,128)(2,1)S(1)}, u32[]{:S(2)}, u32[]{:S(2)}) collective-permute-start(bf16[112,128]{1,0:T(8,128)(2,1)S(1)} %get-tuple-element.59), channel_id=1, source_target_pairs={{0,3},{1,2},{2,1},{3,0},{4,7},{5,6},{6,5},{7,4},{8,11},{9,10},{10,... | collective-permute-start | bytes 86024 | tf_op jit(solution)/shard_map/ppermute | solution.py:356
  65.4 4.8 %collective-permute-start.17 = (bf16[112,128]{1,0:T(8,128)(2,1)S(1)}, bf16[112,128]{1,0:T(8,128)(2,1)S(1)}, u32[]{:S(2)}, u32[]{:S(2)}) collective-permute-start(bf16[112,128]{1,0:T(8,128)(2,1)S(1)} %get-tuple-element.60), channel_id=1, source_target_pairs={{0,2},{1,3},{2,0},{3,1},{4,6},{5,7},{6,4},{7,5},{8,10},{9,11},{10,... | collective-permute-start | bytes 86024 | tf_op jit(solution)/shard_map/ppermute | solution.py:356
  65.4 4.8 %collective-permute-start.18 = (bf16[112,128]{1,0:T(8,128)(2,1)S(1)}, bf16[112,128]{1,0:T(8,128)(2,1)S(1)}, u32[]{:S(2)}, u32[]{:S(2)}) collective-permute-start(bf16[112,128]{1,0:T(8,128)(2,1)S(1)} %get-tuple-element.61), channel_id=1, source_target_pairs={{0,1},{1,0},{2,3},{3,2},{4,5},{5,4},{6,7},{7,6},{8,9},{9,8},{10,11... | collective-permute-start | bytes 86024 | tf_op jit(solution)/shard_map/ppermute | solution.py:356
  70.2 5.7 %collective-permute-start.21 = (bf16[112,128]{1,0:T(8,128)(2,1)S(1)}, bf16[112,128]{1,0:T(8,128)(2,1)S(1)}, u32[]{:S(2)}, u32[]{:S(2)}) collective-permute-start(bf16[112,128]{1,0:T(8,128)(2,1)S(1)} %filt_sum.1.refs_0_), channel_id=1, source_target_pairs={{0,3},{1,2},{2,1},{3,0},{4,7},{5,6},{6,5},{7,4},{8,11},{9,10},{10,... | collective-permute-start | bytes 86024 | tf_op jit(solution)/shard_map/ppermute | solution.py:356
  72.2 5.1 %collective-permute-start.20 = (bf16[112,128]{1,0:T(8,128)(2,1)S(1)}, bf16[112,128]{1,0:T(8,128)(2,1)S(1)}, u32[]{:S(2)}, u32[]{:S(2)}) collective-permute-start(bf16[112,128]{1,0:T(8,128)(2,1)S(1)} %filt_sum.1.refs_0_), channel_id=1, source_target_pairs={{0,2},{1,3},{2,0},{3,1},{4,6},{5,7},{6,4},{7,5},{8,10},{9,11},{10,... | collective-permute-start | bytes 86024 | tf_op jit(solution)/shard_map/ppermute | solution.py:356
  72.9 4.4 %collective-permute-start.19 = (bf16[112,128]{1,0:T(8,128)(2,1)S(1)}, bf16[112,128]{1,0:T(8,128)(2,1)S(1)}, u32[]{:S(2)}, u32[]{:S(2)}) collective-permute-start(bf16[112,128]{1,0:T(8,128)(2,1)S(1)} %filt_sum.1.refs_0_), channel_id=1, source_target_pairs={{0,1},{1,0},{2,3},{3,2},{4,5},{5,4},{6,7},{7,6},{8,9},{9,8},{10,11... | collective-permute-start | bytes 86024 | tf_op jit(solution)/shard_map/ppermute | solution.py:356
  77.3 6.5 %collective-permute-start.24 = (bf16[672,128]{1,0:T(8,128)(2,1)S(1)}, bf16[672,128]{1,0:T(8,128)(2,1)S(1)}, u32[]{:S(2)}, u32[]{:S(2)}) collective-permute-start(bf16[672,128]{1,0:T(8,128)(2,1)S(1)} %line_up.1.refs_0_), channel_id=1, source_target_pairs={{0,24},{4,28},{8,16},{12,20},{16,8},{20,12},{24,0},{28,4},{1,25},{... | collective-permute-start | bytes 516104 | tf_op jit(solution)/shard_map/ppermute | solution.py:356
  79.0 6.5 %collective-permute-start.23 = (bf16[672,128]{1,0:T(8,128)(2,1)S(1)}, bf16[672,128]{1,0:T(8,128)(2,1)S(1)}, u32[]{:S(2)}, u32[]{:S(2)}) collective-permute-start(bf16[672,128]{1,0:T(8,128)(2,1)S(1)} %line_up.1.refs_0_), channel_id=1, source_target_pairs={{0,16},{4,20},{8,24},{12,28},{16,0},{20,4},{24,8},{28,12},{1,17},{... | collective-permute-start | bytes 516104 | tf_op jit(solution)/shard_map/ppermute | solution.py:356
  80.3 5.4 %collective-permute-start.22 = (bf16[672,128]{1,0:T(8,128)(2,1)S(1)}, bf16[672,128]{1,0:T(8,128)(2,1)S(1)}, u32[]{:S(2)}, u32[]{:S(2)}) collective-permute-start(bf16[672,128]{1,0:T(8,128)(2,1)S(1)} %line_up.1.refs_0_), channel_id=1, source_target_pairs={{0,8},{4,12},{8,0},{12,4},{16,24},{20,28},{24,16},{28,20},{1,9},{5... | collective-permute-start | bytes 516104 | tf_op jit(solution)/shard_map/ppermute | solution.py:356
  85.8 2.2 %collective-permute-start.25 = (bf16[4,672,128]{2,1,0:T(8,128)(2,1)S(1)}, bf16[4,672,128]{2,1,0:T(8,128)(2,1)S(1)}, u32[]{:S(2)}, u32[]{:S(2)}) collective-permute-start(bf16[4,672,128]{2,1,0:T(8,128)(2,1)S(1)} %stack.1.pieces), channel_id=1, source_target_pairs={{0,4},{4,0},{8,12},{12,8},{16,20},{20,16},{24,28},{28,24},{1,5},{5... | collective-permute-start | bytes 2064392 | tf_op jit(solution)/shard_map/ppermute | solution.py:501
where the time goes:
time: 89.6 us; the launch traced here: 89.3 us
  starting transfers between devices  43.2 us (48%)
  waiting for transfers between devices  28.4 us (32%)
  Pallas kernels  15.9 us (18%)
  between operations  1 us (1%)
    ppermute x18, starting transfers between devices, paired(): lax.ppermute(values[j], axis, [(i, i ^ step * j) for i in range(count)])  26.4 us
    ppermute x18, waiting for transfers between devices, paired(): lax.ppermute(values[j], axis, [(i, i ^ step * j) for i in range(count)])  25.9 us
    pallas_call x14, Pallas kernels, call(): pl.pallas_call(body, name=name, out_shape=out_shape, in_specs=[HBM if i i...  15.9 us
    ppermute x3, starting transfers between devices, both_sides(): lax.ppermute(high, axis, forward)  12.8 us
    ppermute x3, starting transfers between devices, both_sides(): lax.ppermute(low, axis, backward)  3.86 us
  transfers between devices with their start and end apart: 26, of which 17 were waited for; matrix products, arithmetic and copies ran while one was open for 0% of the time, Pallas kernels for 5%

commit v1 on v0

--- a/solution.py
+++ b/solution.py
@@ -44,51 +44,44 @@
     return 1.0 / (1.0 + jnp.exp(-value))
 
 
-def sides_body(ylo, yhi, sides):
-    sides[:, 0:1] = ylo[...]
-    sides[:, 1:2] = yhi[...]
-
-
-def early_body(
-    volume, xlo, xhi, ylo, yhi, clo, chi, w, windows, sg, pooled, center, field, wide, sem, wsem
-):
-    nx, ny, nz, cin = volume.shape
-    cout = w.shape[3]
+def sides_body(even_pair, odd_pair, sides):
+    even = lax.rem(lax.axis_index("filt"), 2) == 0
+    sides[:, 0:1] = jnp.where(even, odd_pair[:, 1:2], even_pair[:, 1:2])
+    sides[:, 1:2] = jnp.where(even, even_pair[:, 0:1], odd_pair[:, 0:1])
+
+
+def early_body(center, xeven, xodd, mid, ceven, codd, w, windows, sg, pooled, field, wide):
+    nx, ny, nz, cin = center.shape
+    cout = w.shape[2]
     half = nz // 2
     rows = ny * half
     ext = nx + 6
     space = lax.axis_size("space")
-    fetch = pltpu.make_async_copy(volume, center, sem.at[0])
-    fetch.start()
-    weights = [
-        pltpu.make_async_copy(
-            w.at[pl.ds(3 * a, 3), tap],
-            wide.at[
-                pl.ds(3 * a, 3),
-                pl.ds((tap + side) * cin, cin),
-                pl.ds(side * cout, cout),
-            ],
-            wsem.at[a, 2 * tap + side],
-        )
-        for a in range(3)
-        for tap in range(3)
-        for side in range(2)
-    ]
-    for copy in weights:
-        copy.start()
-    wide[:, 0:cin, cout:] = jnp.zeros((9, cin, cout), BF16)
-    wide[:, 3 * cin :, :cout] = jnp.zeros((9, cin, cout), BF16)
+    for ab in range(9):
+        for group in range(4):
+            for side in range(2):
+                tap = group - side
+                value = w[3 * ab + tap] if 0 <= tap <= 2 else jnp.zeros((cin, cout), BF16)
+                wide[
+                    ab, group * cin : (group + 1) * cin, side * cout : (side + 1) * cout
+                ] = value
     field[:, :, 0:8] = jnp.zeros((ext, ny + 2, 8, cin), F32)
     field[:, :, 8 + nz : 16 + nz] = jnp.zeros((ext, ny + 2, 8, cin), F32)
     cells = slice(8, 8 + nz)
-    for top, size, main, sides in ((0, 3, xlo, clo), (nx + 3, 3, xhi, chi)):
-        first = nx - 3 if top == 0 else 0
-        field[top : top + size, 1 : ny + 1, cells] = main[first : first + size].astype(F32)
-        field[top : top + size, 0:1, cells] = sides[first : first + size, 0:1].astype(F32)
-        field[top : top + size, ny + 1 :, cells] = sides[first : first + size, 1:2].astype(F32)
-    field[3 : nx + 3, 0:1, cells] = ylo[...].astype(F32)
-    field[3 : nx + 3, ny + 1 :, cells] = yhi[...].astype(F32)
-    fetch.wait()
+    even = lax.rem(lax.axis_index("space"), 2) == 0
+    for top, first, main, edge in (
+        (0, nx - 3, (xodd, xeven), (codd, ceven)),
+        (nx + 3, 0, (xeven, xodd), (ceven, codd)),
+    ):
+        take = slice(first, first + 3)
+        field[top : top + 3, 1 : ny + 1, cells] = jnp.where(
+            even, main[0][take].astype(F32), main[1][take].astype(F32)
+        )
+        beside = jnp.where(even, edge[0][take].astype(F32), edge[1][take].astype(F32))
+        field[top : top + 3, 0:1, cells] = beside[:, 0:1]
+        field[top : top + 3, ny + 1 :, cells] = beside[:, 1:2]
+    field[3 : nx + 3, 0:1, cells] = mid[:, 0:1].astype(F32)
+    field[3 : nx + 3, ny + 1 :, cells] = mid[:, 1:2].astype(F32)
     field[3 : nx + 3, 1 : ny + 1, cells] = center[...].astype(F32)
     for x in range(ext):
         for group in range(4):
@@ -104,9 +97,6 @@
         acc = jnp.zeros((2 * rows, 2 * cout), F32)
         for ab in range(9):
             a, b = ab // 3, ab % 3
-            if chunk == 0 and b == 0:
-                for copy in weights[6 * a : 6 * a + 6]:
-                    copy.wait()
             left = windows[b, start + a : start + a + 2].reshape(2 * rows, 4 * cin)
             acc = acc + jnp.dot(left, wide[ab], preferred_element_type=F32)
         sig = sigmoid(acc)
@@ -150,21 +140,20 @@
 
 def deep_body(parts_n, *refs):
     parts = refs[:parts_n]
-    wt, cotangent = refs[parts_n : parts_n + 2]
+    wt, cot = refs[parts_n : parts_n + 2]
     block_out, grad, windows = refs[parts_n + 2 : parts_n + 5]
     sends = refs[parts_n + 5 : 2 * parts_n + 5]
-    field, terms, wide, cot, sem = refs[2 * parts_n + 5 :]
+    field, wide, slopes, turned, terms = refs[2 * parts_n + 5 :]
     nx, ny, nz, filters = cot.shape
-    width = wt.shape[3]
-    copies = [
-        pltpu.make_async_copy(wt.at[:, c], wide.at[:, :, pl.ds(c * width, width)], sem.at[c])
-        for c in range(3)
-    ] + [pltpu.make_async_copy(cotangent, cot, sem.at[3])]
-    for copy in copies:
-        copy.start()
+    width = wt.shape[2]
     rows = ny * nz
     py = ny // parts_n
     mine = lax.axis_index("filt")
+    for ab in range(9):
+        for c in range(3):
+            wide[ab, :, c * width : (c + 1) * width] = wt[
+                ab, c * filters : (c + 1) * filters
+            ]
     field[:, 0:1] = jnp.zeros((nx + 2, 1, nz, width), F32)
     field[:, ny + 1 : ny + 2] = jnp.zeros((nx + 2, 1, nz, width), F32)
     for j in range(parts_n):
@@ -178,8 +167,8 @@
                 windows[b, x, :, c * width : (c + 1) * width] = (
                     moved[b : b + ny].reshape(rows, width).astype(BF16)
                 )
-    for copy in copies:
-        copy.wait()
+    slopes[:, 0:1] = jnp.zeros((nx, 1, nz, filters), F32)
+    slopes[:, ny + 1 :] = jnp.zeros((nx, 1, nz, filters), F32)
     for x in range(nx):
         acc = jnp.zeros((rows, filters), F32)
         for ab in range(9):
@@ -190,19 +179,27 @@
         sig = sigmoid(acc)
         block_out[x] = (acc * sig).reshape(ny, nz, filters).astype(BF16)
         slope = sig * (1.0 + acc * (1.0 - sig))
-        grad[x] = (cot[x].astype(F32).reshape(rows, filters) * slope).astype(BF16)
-    terms[...] = jnp.zeros(terms.shape, F32)
-    for ab in range(9):
-        a, b = ab // 3, ab % 3
-        for x in range(nx):
-            part = jnp.dot(grad[x], wide[ab], preferred_element_type=F32)
-            terms[x + a, b : b + ny] += part.reshape(ny, nz, 3 * width)
+        value = (cot[x].astype(F32).reshape(rows, filters) * slope).astype(BF16)
+        grad[x] = value
+        slopes[x, 1 : ny + 1] = value.astype(F32).reshape(ny, nz, filters)
+    for x in range(nx):
+        plane = slopes[x]
+        plane = jnp.concatenate([roll_z(plane, -1), plane, roll_z(plane, 1)], axis=2)
+        for b in range(3):
+            turned[b, x] = (
+                plane[2 - b : 2 - b + ny].reshape(rows, 3 * filters).astype(BF16)
+            )
+    for r in range(nx + 2):
+        total = jnp.zeros((rows, width), F32)
+        for ab in range(9):
+            a, b = ab // 3, ab % 3
+            if 0 <= r - a < nx:
+                total = total + jnp.dot(turned[b, r - a], wt[ab], preferred_element_type=F32)
+        terms[r] = total.reshape(ny, nz, width)
     for j in range(parts_n):
-        spot = lax.bitwise_xor(mine, j) * py + 1
+        spot = lax.bitwise_xor(mine, j) * py
         value = terms[:, pl.ds(spot, py)]
-        total = value[..., width : 2 * width]
-        total = total + roll_z(value[..., :width], -1) + roll_z(value[..., 2 * width :], 1)
-        sends[j][...] = total.reshape(nx + 2, py * nz, width).astype(sends[j].dtype)
+        sends[j][...] = value.reshape(nx + 2, py * nz, width).astype(sends[j].dtype)
 
 
 def deep_grad_body(windows, grad, theirs, mine, held):
@@ -363,11 +360,16 @@
     return [values[0]] + values[:0:-1]
 
 
-def both_sides(low, high, axis):
+def neighbours(value, axis):
     count = lax.axis_size(axis)
-    forward = [(i, i + 1) for i in range(count - 1)]
-    backward = [(i + 1, i) for i in range(count - 1)]
-    return lax.ppermute(high, axis, forward), lax.ppermute(low, axis, backward)
+    return [
+        lax.ppermute(
+            value,
+            axis,
+            [pair for i in range(first, count - 1, 2) for pair in ((i, i + 1), (i + 1, i))],
+        )
+        for first in (0, 1)
+    ]
 
 
 def shards(volume, w_early, w_deep, cotangent):
@@ -380,17 +382,18 @@
     half = nz // 2
     ext = nx + 6
     rows = ny * half
-    ylo, yhi = both_sides(volume[:, :1], volume[:, ny - 1 :], "filt")
-    xlo, xhi = both_sides(volume, volume, "space")
+    edges = jnp.concatenate([volume[:, :1], volume[:, ny - 1 :]], axis=1)
+    yeven, yodd = neighbours(edges, "filt")
+    xeven, xodd = neighbours(volume, "space")
     sides = call(
         sides_body,
         "sides",
         struct((nx, 2, nz, cin)),
-        (ylo, yhi),
+        (yeven, yodd),
         flops=1 << 32,
         moved=1 << 24,
     )
-    clo, chi = both_sides(sides, sides, "space")
+    ceven, codd = neighbours(sides, "space")
     windows, sg, pooled = call(
         early_body,
         "early_conv",
@@ -399,16 +402,12 @@
             struct((nx + 4, rows, 2 * width), F32),
             struct((nx // 2 + 2, rows // 2, width)),
         ),
-        (volume, xlo, xhi, ylo, yhi, clo, chi, w_early.reshape(9, 3, cin, width)),
+        (volume, xeven, xodd, sides, ceven, codd, w_early),
         [
-            pltpu.VMEM(volume.shape, BF16),
             pltpu.VMEM((ext, ny + 2, nz + 16, cin), F32),
             pltpu.VMEM((9, 4 * cin, 2 * width), BF16),
-            DMA((1,)),
-            DMA((3, 6)),
         ],
         flops=2 * (nx + 4) * rows * 36 * cin * 2 * width,
-        hbm=(0, 7),
     )
     parts = paired([pooled] * filt, "filt")
     turned = call(
@@ -432,15 +431,14 @@
             struct((px, prow, width), F32),
         ]
         + [struct((px, prow, width))] * (filt - 1),
-        (*parts, jnp.swapaxes(w_deep, 1, 2).reshape(9, 3, filters, width), cotangent),
+        (*parts, jnp.swapaxes(w_deep, 1, 2).reshape(9, 3 * filters, width), cotangent),
         [
             pltpu.VMEM((px, dy + 2, dz, width), F32),
-            pltpu.VMEM((px, dy + 2, dz, 3 * width), F32),
             pltpu.VMEM((9, filters, 3 * width), BF16),
-            pltpu.VMEM(cotangent.shape, BF16),
-            DMA((4,)),
+            pltpu.VMEM((dx, dy + 2, dz, filters), F32),
+            pltpu.VMEM((3, dx, dy * dz, 3 * filters), BF16),
+            pltpu.VMEM((px, dy, dz, width), F32),
         ],
-        hbm=(filt, filt + 1),
         flops=4 * dx * dy * dz * 27 * width * filters,
     )
     block_out, grad, deep_windows = deep[:3]

time: 89.6 us -> 82 us (0.915)
  starting transfers between devices: 43.2 us -> 39.4 us
  Pallas kernels: 15.9 us -> 12.8 us
    pallas_call x14, Pallas kernels: 15.9 us -> 12.8 us  [call(): pl.pallas_call(body, name=name, out_shape=out_shape, in_specs=[HBM if i i...]
    ppermute x6, starting transfers between devices: 16.7 us -> 13.9 us  [neighbours(): lax.ppermute(value, axis, [pair for i in range(first, count - 1, 2) for p...]
    ppermute x18, starting transfers between devices: 26.4 us -> 25.4 us  [paired(): lax.ppermute(values[j], axis, [(i, i ^ step * j) for i in range(count)])]
  transfers between devices with their start and end apart: 26 -> 26, of which waited for: 17 -> 18; matrix products, arithmetic and copies ran while one was open for 0% -> 0% of each run, Pallas kernels for 5% -> 5%
where the time goes in v1:
time: 82 us; the launch traced here: 81.8 us
  starting transfers between devices  39.4 us (48%)
  waiting for transfers between devices  28.1 us (34%)
  Pallas kernels  12.8 us (16%)
    ppermute x18, waiting for transfers between devices, paired(): lax.ppermute(values[j], axis, [(i, i ^ step * j) for i in range(count)])  25.6 us
    ppermute x18, starting transfers between devices, paired(): lax.ppermute(values[j], axis, [(i, i ^ step * j) for i in range(count)])  25.4 us
    ppermute x6, starting transfers between devices, neighbours(): lax.ppermute(value, axis, [pair for i in range(first, count - 1, 2) for p...  13.9 us
    pallas_call x14, Pallas kernels, call(): pl.pallas_call(body, name=name, out_shape=out_shape, in_specs=[HBM if i i...  12.8 us
  transfers between devices with their start and end apart: 26, of which 18 were waited for; matrix products, arithmetic and copies ran while one was open for 0% of the time, Pallas kernels for 5%

profile of v1, /device:TPU:0, one launch (start us, length us, event | category | flops | bytes accessed | tf_op | source)
XLA Modules:
  0.0 81.8 jit_solution(17784188808139008721)
XLA Ops:
  0.6 0.7 fusion
  1.4 0.8 collective-permute-start.3
  2.2 5.9 %collective-permute-start.2 = (bf16[4,2,16,128]{3,2,1,0:T(8,128)(2,1)S(1)}, bf16[4,2,16,128]{3,2,1,0:T(8,128)(2,1)S(1)}, u32[]{:S(2)}, u32[]{:S(2)}) collective-permute-start(bf16[4,2,16,128]{3,2,1,0:T(8,128)(2,1)S(1)} %pad_maximum_fusion), channel_id=1, source_target_pairs={{0,1},{1,0},{2,3},{3,2},{4,5},{5,4},{6,7},{7,6},{8,9},{9,8},{10,11... | collective-permute-start | bytes 98312 | tf_op jit(solution)/shard_map/ppermute | solution.py:366
  8.1 0.7 collective-permute-start.1
  8.8 2.9 %collective-permute-start = (bf16[4,16,16,128]{3,2,1,0:T(8,128)(2,1)}, bf16[4,16,16,128]{3,2,1,0:T(8,128)(2,1)S(1)}, u32[]{:S(2)}, u32[]{:S(2)}) collective-permute-start(bf16[4,16,16,128]{3,2,1,0:T(8,128)(2,1)} %center.1), channel_id=1, source_target_pairs={{0,4},{4,0},{8,12},{12,8},{16,20},{20,16},{24,28},{28,24},{1,5},{5... | collective-permute-start | bytes 786440 | tf_op jit(solution)/shard_map/ppermute | solution.py:366
  11.7 0.7 collective-permute-start.5
  12.4 2.9 %collective-permute-start.4 = (bf16[4,2,16,128]{3,2,1,0:T(8,128)(2,1)S(1)}, bf16[4,2,16,128]{3,2,1,0:T(8,128)(2,1)S(1)}, u32[]{:S(2)}, u32[]{:S(2)}) collective-permute-start(bf16[4,2,16,128]{3,2,1,0:T(8,128)(2,1)S(1)} %sides.1.mid), channel_id=1, source_target_pairs={{0,4},{4,0},{8,12},{12,8},{16,20},{20,16},{24,28},{28,24},{1,5},{5... | collective-permute-start | bytes 98312 | tf_op jit(solution)/shard_map/ppermute | solution.py:366
  15.3 0.9 %collective-permute-done.4.ceven = bf16[4,2,16,128]{3,2,1,0:T(8,128)(2,1)S(1)} collective-permute-done((bf16[4,2,16,128]{3,2,1,0:T(8,128)(2,1)S(1)}, bf16[4,2,16,128]{3,2,1,0:T(8,128)(2,1)S(1)}, u32[]{:S(2)}, u32[]{:S(2)}) %collective-permute-start.4) | collective-permute-done | bytes 32800 | tf_op jit(solution)/shard_map/ppermute | solution.py:366
  16.2 3.4 %early_conv.1 = (bf16[3,10,128,512]{3,2,1,0:T(8,128)(2,1)S(1)}, f32[8,128,256]{2,1,0:T(8,128)S(1)}, bf16[4,64,128]{2,1,0:T(8,128)(2,1)S(1)}) custom-call(bf16[4,16,16,128]{3,2,1,0:T(8,128)(2,1)S(1)} %copy-done, bf16[4,16,16,128]{3,2,1,0:T(8,128)(2,1)S(1)} %collective-permute-done.xeven, bf16[4,16,16,128]{3,2,1,0:T(8,128)(2,1)S(1)} %collective-permute-done.1.xodd, ...), custom_call_target="tpu_custom_call" | custom-call | flops 2415919104 | bytes 1048576 | tf_op jit(solution)/shard_map/early_conv/pallas_call | solution.py:22
  19.6 1.4 %collective-permute-start.8 = (bf16[4,64,128]{2,1,0:T(8,128)(2,1)S(1)}, bf16[4,64,128]{2,1,0:T(8,128)(2,1)S(1)}, u32[]{:S(2)}, u32[]{:S(2)}) collective-permute-start(bf16[4,64,128]{2,1,0:T(8,128)(2,1)S(1)} %get-tuple-element.37.refs_0_), channel_id=1, source_target_pairs={{0,3},{1,2},{2,1},{3,0},{4,7},{5,6},{6,5},{7,4},{8,11},{9,10},{10,... | collective-permute-start | bytes 196616 | tf_op jit(solution)/shard_map/ppermute | solution.py:353
  21.0 0.4 collective-permute-start.7
  21.5 2.6 %collective-permute-start.6 = (bf16[4,64,128]{2,1,0:T(8,128)(2,1)S(1)}, bf16[4,64,128]{2,1,0:T(8,128)(2,1)S(1)}, u32[]{:S(2)}, u32[]{:S(2)}) collective-permute-start(bf16[4,64,128]{2,1,0:T(8,128)(2,1)S(1)} %get-tuple-element.37.refs_0_), channel_id=1, source_target_pairs={{0,1},{1,0},{2,3},{3,2},{4,5},{5,4},{6,7},{7,6},{8,9},{9,8},{10,11... | collective-permute-start | bytes 196616 | tf_op jit(solution)/shard_map/ppermute | solution.py:353
  24.1 1.1 %turn_windows.1.refs_5_.turned = bf16[3,2,256,1280]{3,2,1,0:T(8,128)(2,1)S(1)} custom-call(bf16[3,10,128,512]{3,2,1,0:T(8,128)(2,1)S(1)} %get-tuple-element.36.windows), custom_call_target="tpu_custom_call" | custom-call | flops 1073741824 | bytes 1048576 | tf_op jit(solution)/shard_map/turn_windows/pallas_call | solution.py:22
  25.2 0.6 collective-permute-done.8.refs_3_
  25.8 3.4 %collective-permute-done.7.refs_2_ = bf16[4,64,128]{2,1,0:T(8,128)(2,1)S(1)} collective-permute-done((bf16[4,64,128]{2,1,0:T(8,128)(2,1)S(1)}, bf16[4,64,128]{2,1,0:T(8,128)(2,1)S(1)}, u32[]{:S(2)}, u32[]{:S(2)}) %collective-permute-start.7) | collective-permute-done | bytes 65568 | tf_op jit(solution)/shard_map/ppermute | solution.py:353
  29.2 2.1 %deep_conv.1 = (bf16[2,32,8,64]{3,2,1,0:T(8,128)(2,1)}, bf16[2,256,64]{2,1,0:T(8,128)(2,1)S(1)}, bf16[3,4,256,384]{3,2,1,0:T(8,128)(2,1)S(1)}, f32[4,64,128]{2,1...) custom-call(bf16[4,64,128]{2,1,0:T(8,128)(2,1)S(1)} %get-tuple-eleme, ...), custom_call_target="tpu_custom_call" | custom-call | flops 452984832 | bytes 1048576 | tf_op jit(solution)/shard_map/deep_conv/pallas_call | solution.py:22
  31.3 1.4 %collective-permute-start.9 = (bf16[4,64,128]{2,1,0:T(8,128)(2,1)S(1)}, bf16[4,64,128]{2,1,0:T(8,128)(2,1)S(1)}, u32[]{:S(2)}, u32[]{:S(2)}) collective-permute-start(bf16[4,64,128]{2,1,0:T(8,128)(2,1)S(1)} %get-tuple-element.43), channel_id=1, source_target_pairs={{0,3},{1,2},{2,1},{3,0},{4,7},{5,6},{6,5},{7,4},{8,11},{9,10},{10,... | collective-permute-start | bytes 196616 | tf_op jit(solution)/shard_map/ppermute | solution.py:353
  32.7 3.0 %collective-permute-start.11 = (bf16[4,64,128]{2,1,0:T(8,128)(2,1)S(1)}, bf16[4,64,128]{2,1,0:T(8,128)(2,1)S(1)}, u32[]{:S(2)}, u32[]{:S(2)}) collective-permute-start(bf16[4,64,128]{2,1,0:T(8,128)(2,1)S(1)} %get-tuple-element.45), channel_id=1, source_target_pairs={{0,1},{1,0},{2,3},{3,2},{4,5},{5,4},{6,7},{7,6},{8,9},{9,8},{10,11... | collective-permute-start | bytes 196616 | tf_op jit(solution)/shard_map/ppermute | solution.py:353
  35.8 0.7 deep_grad.1
  36.5 1.7 %collective-permute-done.9.refs_1_ = bf16[4,64,128]{2,1,0:T(8,128)(2,1)S(1)} collective-permute-done((bf16[4,64,128]{2,1,0:T(8,128)(2,1)S(1)}, bf16[4,64,128]{2,1,0:T(8,128)(2,1)S(1)}, u32[]{:S(2)}, u32[]{:S(2)}) %collective-permute-start.9) | collective-permute-done | bytes 65568 | tf_op jit(solution)/shard_map/ppermute | solution.py:353
  38.2 1.9 %collective-permute-done.10.refs_2_ = bf16[4,64,128]{2,1,0:T(8,128)(2,1)S(1)} collective-permute-done((bf16[4,64,128]{2,1,0:T(8,128)(2,1)S(1)}, bf16[4,64,128]{2,1,0:T(8,128)(2,1)S(1)}, u32[]{:S(2)}, u32[]{:S(2)}) %collective-permute-start.10) | collective-permute-done | bytes 65568 | tf_op jit(solution)/shard_map/ppermute | solution.py:353
  40.1 1.4 %early_grad.1 = (bf16[4,656,128]{2,1,0:T(8,128)(2,1)S(1)}, bf16[8,128,256]{2,1,0:T(8,128)(2,1)S(1)}) custom-call(f32[4,64,128]{2,1,0:T(8,128)S(1)} %get-tuple-element.42.refs_0_, bf16[4,64,128]{2,1,0:T(8,128)(2,1)S(1)} %collective-permute-done.9.refs_1_, bf16[4,64,128]{2,1,0:T(8,128)(2,1)S(1)} %collective-permute-done.10.refs_2_, ...), custom_call_target="tpu_custom_call" | custom-call | flops 1207959552 | bytes 1048576 | tf_op jit(solution)/shard_map/early_grad/pallas_call | solution.py:22
  41.6 1.4 %early_grad_rest.1.mine = f32[4,656,128]{2,1,0:T(8,128)S(1)} custom-call(bf16[8,128,256]{2,1,0:T(8,128)(2,1)S(1)} %get-tuple-element.51.grad, bf16[3,2,256,1280]{3,2,1,0:T(8,128)(2,1)S(1)} %turn_windows.1.refs_5_.turned, f32[4,224,128]{2,1,0:T(8,128)S(1)} %get-tuple-element.52.deep), custom_call_target="tpu_custom_call" | custom-call | flops 1207959552 | bytes 1048576 | tf_op jit(solution)/shard_map/early_grad_rest/pallas_call | solution.py:22
  43.0 0.7 collective-permute-done.12.other
  43.8 2.1 %collective-permute-start.13 = (bf16[656,128]{1,0:T(8,128)(2,1)S(1)}, bf16[656,128]{1,0:T(8,128)(2,1)S(1)}, u32[]{:S(2)}, u32[]{:S(2)}) collective-permute-start(bf16[656,128]{1,0:T(8,128)(2,1)S(1)} %get-tuple-element.55), channel_id=1, source_target_pairs={{0,24},{4,28},{8,16},{12,20},{16,8},{20,12},{24,0},{28,4},{1,25},{... | collective-permute-start | bytes 503816 | tf_op jit(solution)/shard_map/ppermute | solution.py:353
  46.0 1.9 %collective-permute-start.14 = (bf16[656,128]{1,0:T(8,128)(2,1)S(1)}, bf16[656,128]{1,0:T(8,128)(2,1)S(1)}, u32[]{:S(2)}, u32[]{:S(2)}) collective-permute-start(bf16[656,128]{1,0:T(8,128)(2,1)S(1)} %get-tuple-element.56), channel_id=1, source_target_pairs={{0,16},{4,20},{8,24},{12,28},{16,0},{20,4},{24,8},{28,12},{1,17},{... | collective-permute-start | bytes 503816 | tf_op jit(solution)/shard_map/ppermute | solution.py:353
  47.8 4.1 %collective-permute-done.13.refs_1_ = bf16[656,128]{1,0:T(8,128)(2,1)S(1)} collective-permute-done((bf16[656,128]{1,0:T(8,128)(2,1)S(1)}, bf16[656,128]{1,0:T(8,128)(2,1)S(1)}, u32[]{:S(2)}, u32[]{:S(2)}) %collective-permute-start.13) | collective-permute-done | bytes 167968 | tf_op jit(solution)/shard_map/ppermute | solution.py:353
  52.0 2.8 %collective-permute-done.14.refs_2_ = bf16[656,128]{1,0:T(8,128)(2,1)S(1)} collective-permute-done((bf16[656,128]{1,0:T(8,128)(2,1)S(1)}, bf16[656,128]{1,0:T(8,128)(2,1)S(1)}, u32[]{:S(2)}, u32[]{:S(2)}) %collective-permute-start.14) | collective-permute-done | bytes 167968 | tf_op jit(solution)/shard_map/ppermute | solution.py:353
  54.7 1.0 %collective-permute-done.15.refs_3_ = bf16[656,128]{1,0:T(8,128)(2,1)S(1)} collective-permute-done((bf16[656,128]{1,0:T(8,128)(2,1)S(1)}, bf16[656,128]{1,0:T(8,128)(2,1)S(1)}, u32[]{:S(2)}, u32[]{:S(2)}) %collective-permute-start.15) | collective-permute-done | bytes 167968 | tf_op jit(solution)/shard_map/ppermute | solution.py:353
  55.8 1.8 %collective-permute-start.16 = (bf16[112,128]{1,0:T(8,128)(2,1)S(1)}, bf16[112,128]{1,0:T(8,128)(2,1)S(1)}, u32[]{:S(2)}, u32[]{:S(2)}) collective-permute-start(bf16[112,128]{1,0:T(8,128)(2,1)S(1)} %get-tuple-element.59), channel_id=1, source_target_pairs={{0,3},{1,2},{2,1},{3,0},{4,7},{5,6},{6,5},{7,4},{8,11},{9,10},{10,... | collective-permute-start | bytes 86024 | tf_op jit(solution)/shard_map/ppermute | solution.py:353
  57.7 0.5 collective-permute-start.17
  58.1 2.2 %collective-permute-start.18 = (bf16[112,128]{1,0:T(8,128)(2,1)S(1)}, bf16[112,128]{1,0:T(8,128)(2,1)S(1)}, u32[]{:S(2)}, u32[]{:S(2)}) collective-permute-start(bf16[112,128]{1,0:T(8,128)(2,1)S(1)} %get-tuple-element.61), channel_id=1, source_target_pairs={{0,1},{1,0},{2,3},{3,2},{4,5},{5,4},{6,7},{7,6},{8,9},{9,8},{10,11... | collective-permute-start | bytes 86024 | tf_op jit(solution)/shard_map/ppermute | solution.py:353
  60.3 1.5 %collective-permute-done.16.refs_1_ = bf16[112,128]{1,0:T(8,128)(2,1)S(1)} collective-permute-done((bf16[112,128]{1,0:T(8,128)(2,1)S(1)}, bf16[112,128]{1,0:T(8,128)(2,1)S(1)}, u32[]{:S(2)}, u32[]{:S(2)}) %collective-permute-start.16) | collective-permute-done | bytes 28704 | tf_op jit(solution)/shard_map/ppermute | solution.py:353
  61.8 0.7 collective-permute-done.17.refs_2_
  62.5 2.1 %collective-permute-start.21 = (bf16[112,128]{1,0:T(8,128)(2,1)S(1)}, bf16[112,128]{1,0:T(8,128)(2,1)S(1)}, u32[]{:S(2)}, u32[]{:S(2)}) collective-permute-start(bf16[112,128]{1,0:T(8,128)(2,1)S(1)} %filt_sum.1.refs_0_), channel_id=1, source_target_pairs={{0,3},{1,2},{2,1},{3,0},{4,7},{5,6},{6,5},{7,4},{8,11},{9,10},{10,... | collective-permute-start | bytes 86024 | tf_op jit(solution)/shard_map/ppermute | solution.py:353
  64.6 1.1 %collective-permute-start.20 = (bf16[112,128]{1,0:T(8,128)(2,1)S(1)}, bf16[112,128]{1,0:T(8,128)(2,1)S(1)}, u32[]{:S(2)}, u32[]{:S(2)}) collective-permute-start(bf16[112,128]{1,0:T(8,128)(2,1)S(1)} %filt_sum.1.refs_0_), channel_id=1, source_target_pairs={{0,2},{1,3},{2,0},{3,1},{4,6},{5,7},{6,4},{7,5},{8,10},{9,11},{10,... | collective-permute-start | bytes 86024 | tf_op jit(solution)/shard_map/ppermute | solution.py:353
  65.7 1.3 %collective-permute-start.19 = (bf16[112,128]{1,0:T(8,128)(2,1)S(1)}, bf16[112,128]{1,0:T(8,128)(2,1)S(1)}, u32[]{:S(2)}, u32[]{:S(2)}) collective-permute-start(bf16[112,128]{1,0:T(8,128)(2,1)S(1)} %filt_sum.1.refs_0_), channel_id=1, source_target_pairs={{0,1},{1,0},{2,3},{3,2},{4,5},{5,4},{6,7},{7,6},{8,9},{9,8},{10,11... | collective-permute-start | bytes 86024 | tf_op jit(solution)/shard_map/ppermute | solution.py:353
  67.0 1.3 %collective-permute-done.21.refs_3_ = bf16[112,128]{1,0:T(8,128)(2,1)S(1)} collective-permute-done((bf16[112,128]{1,0:T(8,128)(2,1)S(1)}, bf16[112,128]{1,0:T(8,128)(2,1)S(1)}, u32[]{:S(2)}, u32[]{:S(2)}) %collective-permute-start.21) | collective-permute-done | bytes 28704 | tf_op jit(solution)/shard_map/ppermute | solution.py:353
  68.3 1.5 %collective-permute-done.20.refs_2_ = bf16[112,128]{1,0:T(8,128)(2,1)S(1)} collective-permute-done((bf16[112,128]{1,0:T(8,128)(2,1)S(1)}, bf16[112,128]{1,0:T(8,128)(2,1)S(1)}, u32[]{:S(2)}, u32[]{:S(2)}) %collective-permute-start.20) | collective-permute-done | bytes 28704 | tf_op jit(solution)/shard_map/ppermute | solution.py:353
  69.9 1.4 %collective-permute-start.24 = (bf16[672,128]{1,0:T(8,128)(2,1)S(1)}, bf16[672,128]{1,0:T(8,128)(2,1)S(1)}, u32[]{:S(2)}, u32[]{:S(2)}) collective-permute-start(bf16[672,128]{1,0:T(8,128)(2,1)S(1)} %line_up.1.refs_0_), channel_id=1, source_target_pairs={{0,24},{4,28},{8,16},{12,20},{16,8},{20,12},{24,0},{28,4},{1,25},{... | collective-permute-start | bytes 516104 | tf_op jit(solution)/shard_map/ppermute | solution.py:353
  71.3 1.4 %collective-permute-start.23 = (bf16[672,128]{1,0:T(8,128)(2,1)S(1)}, bf16[672,128]{1,0:T(8,128)(2,1)S(1)}, u32[]{:S(2)}, u32[]{:S(2)}) collective-permute-start(bf16[672,128]{1,0:T(8,128)(2,1)S(1)} %line_up.1.refs_0_), channel_id=1, source_target_pairs={{0,16},{4,20},{8,24},{12,28},{16,0},{20,4},{24,8},{28,12},{1,17},{... | collective-permute-start | bytes 516104 | tf_op jit(solution)/shard_map/ppermute | solution.py:353
  72.7 0.8 collective-permute-start.22
  73.5 2.9 %collective-permute-done.24.refs_3_ = bf16[672,128]{1,0:T(8,128)(2,1)S(1)} collective-permute-done((bf16[672,128]{1,0:T(8,128)(2,1)S(1)}, bf16[672,128]{1,0:T(8,128)(2,1)S(1)}, u32[]{:S(2)}, u32[]{:S(2)}) %collective-permute-start.24) | collective-permute-done | bytes 172064 | tf_op jit(solution)/shard_map/ppermute | solution.py:353
  76.4 1.7 %collective-permute-done.23.refs_2_ = bf16[672,128]{1,0:T(8,128)(2,1)S(1)} collective-permute-done((bf16[672,128]{1,0:T(8,128)(2,1)S(1)}, bf16[672,128]{1,0:T(8,128)(2,1)S(1)}, u32[]{:S(2)}, u32[]{:S(2)}) %collective-permute-start.23) | collective-permute-done | bytes 172064 | tf_op jit(solution)/shard_map/ppermute | solution.py:353
  78.1 0.3 collective-permute-done.22.refs_1_
  78.6 1.1 %finish_own.1 = (f32[27,128,128]{2,1,0:T(8,128)}, f32[27,64,128]{2,1,0:T(8,128)}) custom-call(bf16[4,672,128]{2,1,0:T(8,128)(2,1)S(1)} %stack.1.pieces), custom_call_target="tpu_custom_call" | custom-call | bytes 1048576 | tf_op jit(solution)/shard_map/finish_own/pallas_call | solution.py:22
  79.7 1.0 %collective-permute-done.25.pieces = bf16[4,672,128]{2,1,0:T(8,128)(2,1)S(1)} collective-permute-done((bf16[4,672,128]{2,1,0:T(8,128)(2,1)S(1)}, bf16[4,672,128]{2,1,0:T(8,128)(2,1)S(1)}, u32[]{:S(2)}, u32[]{:S(2)}) %collective-permute-start.25) | collective-permute-done | bytes 688160 | tf_op jit(solution)/shard_map/ppermute | solution.py:499
  80.7 1.1 %finish_other.1 = (f32[27,128,128]{2,1,0:T(8,128)}, f32[27,64,128]{2,1,0:T(8,128)}) custom-call(bf16[4,672,128]{2,1,0:T(8,128)(2,1)S(1)} %collective-permute-done.25.pieces, f32[27,128,128]{2,1,0:T(8,128)} %get-tuple-element.63.refs_0_, f32[27,64,128]{2,1,0:T(8,128)} %get-tuple-element.64.refs_1_), custom_call_target="tpu_custom_call", output_to_operand_aliasing={{0}: (1, {}), {1}: (2, {})} | custom-call | bytes 1048576 | tf_op jit(solution)/shard_map/finish_other/pallas_call | solution.py:22
  (28 shorter events, 0.7 us)
Async XLA Ops:
  1.4 14.8 %copy-start = (bf16[4,16,16,128]{3,2,1,0:T(8,128)(2,1)S(1)}, bf16[4,16,16,128]{3,2,1,0:T(8,128)(2,1)}, u32[]{:S(2)}) copy-start(bf16[4,16,16,128]{3,2,1,0:T(8,128)(2,1)} %center.1) | copy-start | bytes 786436
  1.4 14.8 %copy-start.1 = (bf16[27,128,128]{2,1,0:T(8,128)(2,1)S(1)}, bf16[27,128,128]{2,1,0:T(8,128)(2,1)}, u32[]{:S(2)}) copy-start(bf16[27,128,128]{2,1,0:T(8,128)(2,1)} %w.1) | copy-start | bytes 2654212
  1.4 10.3 %collective-permute-start.3 = (bf16[4,2,16,128]{3,2,1,0:T(8,128)(2,1)S(1)}, bf16[4,2,16,128]{3,2,1,0:T(8,128)(2,1)S(1)}, u32[]{:S(2)}, u32[]{:S(2)}) collective-permute-start(bf16[4,2,16,128]{3,2,1,0:T(8,128)(2,1)S(1)} %pad_maximum_fusion), channel_id=1, source_target_pairs={{1,2},{2,1},{5,6},{6,5},{9,10},{10,9},{13,14},{14,13},{17,18},{18,... | collective-permute-start | bytes 98312 | tf_op jit(solution)/shard_map/ppermute | solution.py:366
  2.2 9.5 %collective-permute-start.2 = (bf16[4,2,16,128]{3,2,1,0:T(8,128)(2,1)S(1)}, bf16[4,2,16,128]{3,2,1,0:T(8,128)(2,1)S(1)}, u32[]{:S(2)}, u32[]{:S(2)}) collective-permute-start(bf16[4,2,16,128]{3,2,1,0:T(8,128)(2,1)S(1)} %pad_maximum_fusion), channel_id=1, source_target_pairs={{0,1},{1,0},{2,3},{3,2},{4,5},{5,4},{6,7},{7,6},{8,9},{9,8},{10,11... | collective-permute-start | bytes 98312 | tf_op jit(solution)/shard_map/ppermute | solution.py:366
  8.1 8.1 %collective-permute-start.1 = (bf16[4,16,16,128]{3,2,1,0:T(8,128)(2,1)}, bf16[4,16,16,128]{3,2,1,0:T(8,128)(2,1)S(1)}, u32[]{:S(2)}, u32[]{:S(2)}) collective-permute-start(bf16[4,16,16,128]{3,2,1,0:T(8,128)(2,1)} %center.1), channel_id=1, source_target_pairs={{4,8},{8,4},{12,16},{16,12},{20,24},{24,20},{5,9},{9,5},{13,17},{1... | collective-permute-start | bytes 786440 | tf_op jit(solution)/shard_map/ppermute | solution.py:366
  8.8 7.4 %collective-permute-start = (bf16[4,16,16,128]{3,2,1,0:T(8,128)(2,1)}, bf16[4,16,16,128]{3,2,1,0:T(8,128)(2,1)S(1)}, u32[]{:S(2)}, u32[]{:S(2)}) collective-permute-start(bf16[4,16,16,128]{3,2,1,0:T(8,128)(2,1)} %center.1), channel_id=1, source_target_pairs={{0,4},{4,0},{8,12},{12,8},{16,20},{20,16},{24,28},{28,24},{1,5},{5... | collective-permute-start | bytes 786440 | tf_op jit(solution)/shard_map/ppermute | solution.py:366
  11.7 3.6 %collective-permute-start.5 = (bf16[4,2,16,128]{3,2,1,0:T(8,128)(2,1)S(1)}, bf16[4,2,16,128]{3,2,1,0:T(8,128)(2,1)S(1)}, u32[]{:S(2)}, u32[]{:S(2)}) collective-permute-start(bf16[4,2,16,128]{3,2,1,0:T(8,128)(2,1)S(1)} %sides.1.mid), channel_id=1, source_target_pairs={{4,8},{8,4},{12,16},{16,12},{20,24},{24,20},{5,9},{9,5},{13,17},{1... | collective-permute-start | bytes 98312 | tf_op jit(solution)/shard_map/ppermute | solution.py:366
  12.4 3.8 %collective-permute-start.4 = (bf16[4,2,16,128]{3,2,1,0:T(8,128)(2,1)S(1)}, bf16[4,2,16,128]{3,2,1,0:T(8,128)(2,1)S(1)}, u32[]{:S(2)}, u32[]{:S(2)}) collective-permute-start(bf16[4,2,16,128]{3,2,1,0:T(8,128)(2,1)S(1)} %sides.1.mid), channel_id=1, source_target_pairs={{0,4},{4,0},{8,12},{12,8},{16,20},{20,16},{24,28},{28,24},{1,5},{5... | collective-permute-start | bytes 98312 | tf_op jit(solution)/shard_map/ppermute | solution.py:366
  19.6 6.2 %collective-permute-start.8 = (bf16[4,64,128]{2,1,0:T(8,128)(2,1)S(1)}, bf16[4,64,128]{2,1,0:T(8,128)(2,1)S(1)}, u32[]{:S(2)}, u32[]{:S(2)}) collective-permute-start(bf16[4,64,128]{2,1,0:T(8,128)(2,1)S(1)} %get-tuple-element.37.refs_0_), channel_id=1, source_target_pairs={{0,3},{1,2},{2,1},{3,0},{4,7},{5,6},{6,5},{7,4},{8,11},{9,10},{10,... | collective-permute-start | bytes 196616 | tf_op jit(solution)/shard_map/ppermute | solution.py:353
  21.0 8.1 %collective-permute-start.7 = (bf16[4,64,128]{2,1,0:T(8,128)(2,1)S(1)}, bf16[4,64,128]{2,1,0:T(8,128)(2,1)S(1)}, u32[]{:S(2)}, u32[]{:S(2)}) collective-permute-start(bf16[4,64,128]{2,1,0:T(8,128)(2,1)S(1)} %get-tuple-element.37.refs_0_), channel_id=1, source_target_pairs={{0,2},{1,3},{2,0},{3,1},{4,6},{5,7},{6,4},{7,5},{8,10},{9,11},{10,... | collective-permute-start | bytes 196616 | tf_op jit(solution)/shard_map/ppermute | solution.py:353
  21.5 7.7 %collective-permute-start.6 = (bf16[4,64,128]{2,1,0:T(8,128)(2,1)S(1)}, bf16[4,64,128]{2,1,0:T(8,128)(2,1)S(1)}, u32[]{:S(2)}, u32[]{:S(2)}) collective-permute-start(bf16[4,64,128]{2,1,0:T(8,128)(2,1)S(1)} %get-tuple-element.37.refs_0_), channel_id=1, source_target_pairs={{0,1},{1,0},{2,3},{3,2},{4,5},{5,4},{6,7},{7,6},{8,9},{9,8},{10,11... | collective-permute-start | bytes 196616 | tf_op jit(solution)/shard_map/ppermute | solution.py:353
  24.1 5.1 %copy-start.2 = (bf16[27,128,64]{1,2,0:T(8,128)(2,1)S(1)}, bf16[27,128,64]{1,2,0:T(8,128)(2,1)}, u32[]{:S(2)}) copy-start(bf16[27,128,64]{1,2,0:T(8,128)(2,1)} %param.6) | copy-start | bytes 1327108
  24.1 5.1 %copy-start.3 = (bf16[2,32,8,64]{3,2,1,0:T(8,128)(2,1)S(1)}, bf16[2,32,8,64]{3,2,1,0:T(8,128)(2,1)}, u32[]{:S(2)}) copy-start(bf16[2,32,8,64]{3,2,1,0:T(8,128)(2,1)} %refs_5_.1) | copy-start | bytes 196612
  31.3 6.9 %collective-permute-start.9 = (bf16[4,64,128]{2,1,0:T(8,128)(2,1)S(1)}, bf16[4,64,128]{2,1,0:T(8,128)(2,1)S(1)}, u32[]{:S(2)}, u32[]{:S(2)}) collective-permute-start(bf16[4,64,128]{2,1,0:T(8,128)(2,1)S(1)} %get-tuple-element.43), channel_id=1, source_target_pairs={{0,3},{1,2},{2,1},{3,0},{4,7},{5,6},{6,5},{7,4},{8,11},{9,10},{10,... | collective-permute-start | bytes 196616 | tf_op jit(solution)/shard_map/ppermute | solution.py:353
  32.7 7.4 %collective-permute-start.10 = (bf16[4,64,128]{2,1,0:T(8,128)(2,1)S(1)}, bf16[4,64,128]{2,1,0:T(8,128)(2,1)S(1)}, u32[]{:S(2)}, u32[]{:S(2)}) collective-permute-start(bf16[4,64,128]{2,1,0:T(8,128)(2,1)S(1)} %get-tuple-element.44), channel_id=1, source_target_pairs={{0,2},{1,3},{2,0},{3,1},{4,6},{5,7},{6,4},{7,5},{8,10},{9,11},{10,... | collective-permute-start | bytes 196616 | tf_op jit(solution)/shard_map/ppermute | solution.py:353
  32.7 7.4 %collective-permute-start.11 = (bf16[4,64,128]{2,1,0:T(8,128)(2,1)S(1)}, bf16[4,64,128]{2,1,0:T(8,128)(2,1)S(1)}, u32[]{:S(2)}, u32[]{:S(2)}) collective-permute-start(bf16[4,64,128]{2,1,0:T(8,128)(2,1)S(1)} %get-tuple-element.45), channel_id=1, source_target_pairs={{0,1},{1,0},{2,3},{3,2},{4,5},{5,4},{6,7},{7,6},{8,9},{9,8},{10,11... | collective-permute-start | bytes 196616 | tf_op jit(solution)/shard_map/ppermute | solution.py:353
  41.5 2.2 %collective-permute-start.12 = (bf16[4,656,128]{2,1,0:T(8,128)(2,1)S(1)}, bf16[4,656,128]{2,1,0:T(8,128)(2,1)S(1)}, u32[]{:S(2)}, u32[]{:S(2)}) collective-permute-start(bf16[4,656,128]{2,1,0:T(8,128)(2,1)S(1)} %get-tuple-element.53), channel_id=1, source_target_pairs={{0,4},{4,0},{8,12},{12,8},{16,20},{20,16},{24,28},{28,24},{1,5},{5... | collective-permute-start | bytes 2015240 | tf_op jit(solution)/shard_map/ppermute | solution.py:468
  43.8 8.1 %collective-permute-start.13 = (bf16[656,128]{1,0:T(8,128)(2,1)S(1)}, bf16[656,128]{1,0:T(8,128)(2,1)S(1)}, u32[]{:S(2)}, u32[]{:S(2)}) collective-permute-start(bf16[656,128]{1,0:T(8,128)(2,1)S(1)} %get-tuple-element.55), channel_id=1, source_target_pairs={{0,24},{4,28},{8,16},{12,20},{16,8},{20,12},{24,0},{28,4},{1,25},{... | collective-permute-start | bytes 503816 | tf_op jit(solution)/shard_map/ppermute | solution.py:353
  46.0 8.7 %collective-permute-start.14 = (bf16[656,128]{1,0:T(8,128)(2,1)S(1)}, bf16[656,128]{1,0:T(8,128)(2,1)S(1)}, u32[]{:S(2)}, u32[]{:S(2)}) collective-permute-start(bf16[656,128]{1,0:T(8,128)(2,1)S(1)} %get-tuple-element.56), channel_id=1, source_target_pairs={{0,16},{4,20},{8,24},{12,28},{16,0},{20,4},{24,8},{28,12},{1,17},{... | collective-permute-start | bytes 503816 | tf_op jit(solution)/shard_map/ppermute | solution.py:353
  47.8 7.9 %collective-permute-start.15 = (bf16[656,128]{1,0:T(8,128)(2,1)S(1)}, bf16[656,128]{1,0:T(8,128)(2,1)S(1)}, u32[]{:S(2)}, u32[]{:S(2)}) collective-permute-start(bf16[656,128]{1,0:T(8,128)(2,1)S(1)} %get-tuple-element.57), channel_id=1, source_target_pairs={{0,8},{4,12},{8,0},{12,4},{16,24},{20,28},{24,16},{28,20},{1,9},{5... | collective-permute-start | bytes 503816 | tf_op jit(solution)/shard_map/ppermute | solution.py:353
  55.8 6.0 %collective-permute-start.16 = (bf16[112,128]{1,0:T(8,128)(2,1)S(1)}, bf16[112,128]{1,0:T(8,128)(2,1)S(1)}, u32[]{:S(2)}, u32[]{:S(2)}) collective-permute-start(bf16[112,128]{1,0:T(8,128)(2,1)S(1)} %get-tuple-element.59), channel_id=1, source_target_pairs={{0,3},{1,2},{2,1},{3,0},{4,7},{5,6},{6,5},{7,4},{8,11},{9,10},{10,... | collective-permute-start | bytes 86024 | tf_op jit(solution)/shard_map/ppermute | solution.py:353
  57.7 4.8 %collective-permute-start.17 = (bf16[112,128]{1,0:T(8,128)(2,1)S(1)}, bf16[112,128]{1,0:T(8,128)(2,1)S(1)}, u32[]{:S(2)}, u32[]{:S(2)}) collective-permute-start(bf16[112,128]{1,0:T(8,128)(2,1)S(1)} %get-tuple-element.60), channel_id=1, source_target_pairs={{0,2},{1,3},{2,0},{3,1},{4,6},{5,7},{6,4},{7,5},{8,10},{9,11},{10,... | collective-permute-start | bytes 86024 | tf_op jit(solution)/shard_map/ppermute | solution.py:353
  58.1 4.4 %collective-permute-start.18 = (bf16[112,128]{1,0:T(8,128)(2,1)S(1)}, bf16[112,128]{1,0:T(8,128)(2,1)S(1)}, u32[]{:S(2)}, u32[]{:S(2)}) collective-permute-start(bf16[112,128]{1,0:T(8,128)(2,1)S(1)} %get-tuple-element.61), channel_id=1, source_target_pairs={{0,1},{1,0},{2,3},{3,2},{4,5},{5,4},{6,7},{7,6},{8,9},{9,8},{10,11... | collective-permute-start | bytes 86024 | tf_op jit(solution)/shard_map/ppermute | solution.py:353
  62.5 5.7 %collective-permute-start.21 = (bf16[112,128]{1,0:T(8,128)(2,1)S(1)}, bf16[112,128]{1,0:T(8,128)(2,1)S(1)}, u32[]{:S(2)}, u32[]{:S(2)}) collective-permute-start(bf16[112,128]{1,0:T(8,128)(2,1)S(1)} %filt_sum.1.refs_0_), channel_id=1, source_target_pairs={{0,3},{1,2},{2,1},{3,0},{4,7},{5,6},{6,5},{7,4},{8,11},{9,10},{10,... | collective-permute-start | bytes 86024 | tf_op jit(solution)/shard_map/ppermute | solution.py:353
  64.6 5.1 %collective-permute-start.20 = (bf16[112,128]{1,0:T(8,128)(2,1)S(1)}, bf16[112,128]{1,0:T(8,128)(2,1)S(1)}, u32[]{:S(2)}, u32[]{:S(2)}) collective-permute-start(bf16[112,128]{1,0:T(8,128)(2,1)S(1)} %filt_sum.1.refs_0_), channel_id=1, source_target_pairs={{0,2},{1,3},{2,0},{3,1},{4,6},{5,7},{6,4},{7,5},{8,10},{9,11},{10,... | collective-permute-start | bytes 86024 | tf_op jit(solution)/shard_map/ppermute | solution.py:353
  65.7 4.2 %collective-permute-start.19 = (bf16[112,128]{1,0:T(8,128)(2,1)S(1)}, bf16[112,128]{1,0:T(8,128)(2,1)S(1)}, u32[]{:S(2)}, u32[]{:S(2)}) collective-permute-start(bf16[112,128]{1,0:T(8,128)(2,1)S(1)} %filt_sum.1.refs_0_), channel_id=1, source_target_pairs={{0,1},{1,0},{2,3},{3,2},{4,5},{5,4},{6,7},{7,6},{8,9},{9,8},{10,11... | collective-permute-start | bytes 86024 | tf_op jit(solution)/shard_map/ppermute | solution.py:353
  69.9 6.5 %collective-permute-start.24 = (bf16[672,128]{1,0:T(8,128)(2,1)S(1)}, bf16[672,128]{1,0:T(8,128)(2,1)S(1)}, u32[]{:S(2)}, u32[]{:S(2)}) collective-permute-start(bf16[672,128]{1,0:T(8,128)(2,1)S(1)} %line_up.1.refs_0_), channel_id=1, source_target_pairs={{0,24},{4,28},{8,16},{12,20},{16,8},{20,12},{24,0},{28,4},{1,25},{... | collective-permute-start | bytes 516104 | tf_op jit(solution)/shard_map/ppermute | solution.py:353
  71.3 6.8 %collective-permute-start.23 = (bf16[672,128]{1,0:T(8,128)(2,1)S(1)}, bf16[672,128]{1,0:T(8,128)(2,1)S(1)}, u32[]{:S(2)}, u32[]{:S(2)}) collective-permute-start(bf16[672,128]{1,0:T(8,128)(2,1)S(1)} %line_up.1.refs_0_), channel_id=1, source_target_pairs={{0,16},{4,20},{8,24},{12,28},{16,0},{20,4},{24,8},{28,12},{1,17},{... | collective-permute-start | bytes 516104 | tf_op jit(solution)/shard_map/ppermute | solution.py:353
  72.7 5.7 %collective-permute-start.22 = (bf16[672,128]{1,0:T(8,128)(2,1)S(1)}, bf16[672,128]{1,0:T(8,128)(2,1)S(1)}, u32[]{:S(2)}, u32[]{:S(2)}) collective-permute-start(bf16[672,128]{1,0:T(8,128)(2,1)S(1)} %line_up.1.refs_0_), channel_id=1, source_target_pairs={{0,8},{4,12},{8,0},{12,4},{16,24},{20,28},{24,16},{28,20},{1,9},{5... | collective-permute-start | bytes 516104 | tf_op jit(solution)/shard_map/ppermute | solution.py:353
  78.5 2.2 %collective-permute-start.25 = (bf16[4,672,128]{2,1,0:T(8,128)(2,1)S(1)}, bf16[4,672,128]{2,1,0:T(8,128)(2,1)S(1)}, u32[]{:S(2)}, u32[]{:S(2)}) collective-permute-start(bf16[4,672,128]{2,1,0:T(8,128)(2,1)S(1)} %stack.1.pieces), channel_id=1, source_target_pairs={{0,4},{4,0},{8,12},{12,8},{16,20},{20,16},{24,28},{28,24},{1,5},{5... | collective-permute-start | bytes 2064392 | tf_op jit(solution)/shard_map/ppermute | solution.py:499
